TPU v7x, 32 devices: a whole 2x2x4 slice. The times are simulated.
32 devices in a mesh: dp: 16 (over z, x, core), tensor: 2 (over y).
Axes of the slice: x: 2, y: 2, z: 4, core: 2. Of those that a mesh axis runs over, the one named last changes fastest.
Arguments:
- tokens: bfloat16 [16384, 768], P(('dp', 'tensor')), may hold values from -6 to 6
- first_values: bfloat16 [16384, 768], P(('dp', 'tensor')), may hold values from -6 to 6
- lengths: int32 [16], P('dp'), may hold values from 513 to 1024, as said below
- reuse_index: int32 [6], replicated, may hold values from 0 to 11
- ln1_gain: float32 [768], replicated, may hold values from 0.1 to 1.9
- ln1_bias: float32 [768], replicated, may hold values from -1.5 to 1.5
- w_query: bfloat16 [768, 768], P(None, 'tensor'), may hold values from -0.21875 to 0.21875
- query_bias: float32 [768], P('tensor'), may hold values from -2.5 to 2.5
- w_key: bfloat16 [768, 768], P(None, 'tensor'), may hold values from -0.21875 to 0.21875
- w_value: bfloat16 [768, 384], P(None, 'tensor'), may hold values from -0.21875 to 0.21875
- value_bias: float32 [384], P('tensor'), may hold values from -2.5 to 2.5
- w_out: bfloat16 [768, 768], P('tensor'), may hold values from -3.5 to 3.5
- out_bias: float32 [768], replicated, may hold values from -1.5 to 1.5
- ln2_gain: float32 [768], replicated, may hold values from 0.1 to 1.9
- ln2_bias: float32 [768], replicated, may hold values from -1.5 to 1.5
- w_up: bfloat16 [768, 3072], P(None, 'tensor'), may hold values from -0.21875 to 0.21875
- up_bias: float32 [3072], P('tensor'), may hold values from -2.5 to 2.5
- w_down: bfloat16 [3072, 768], P('tensor'), may hold values from -0.109375 to 0.109375
- down_bias: float32 [768], replicated, may hold values from -1.5 to 1.5
- cotangent: bfloat16 [16384, 768], P(('dp', 'tensor')), may hold values from -6 to 6
Outputs:
- layer_out: bfloat16 [16384, 768], P(('dp', 'tensor'))
- tokens_grad: float32 [16384, 768], P(('dp', 'tensor'))
- first_values_grad: float32 [16384, 768], P(('dp', 'tensor'))
- ln1_gain_grad: float32 [768], replicated
- ln1_bias_grad: float32 [768], replicated
- w_query_grad: float32 [768, 768], P(None, 'tensor')
- query_bias_grad: float32 [768], P('tensor')
- w_key_grad: float32 [768, 768], P(None, 'tensor')
- w_value_grad: float32 [768, 384], P(None, 'tensor')
- value_bias_grad: float32 [384], P('tensor')
- w_out_grad: float32 [768, 768], P('tensor')
- out_bias_grad: float32 [768], replicated
- ln2_gain_grad: float32 [768], replicated
- ln2_bias_grad: float32 [768], replicated
- w_up_grad: float32 [768, 3072], P(None, 'tensor')
- up_bias_grad: float32 [3072], P('tensor')
- w_down_grad: float32 [3072, 768], P('tensor')
- down_bias_grad: float32 [768], replicated
Inputs may be any that keep to these rules, and one draw needn't show every extreme that they name: `lengths`: each sequence has more than 512 tokens, and some sequence fills all 1024 slots. `reuse_index`: indices may repeat.
All inputs are finite; a program needn't handle non-finite values.
Results may differ from a plain program's by a relative error of at most 0.015.
Values may be sent and summed in bfloat16 or wider, within the bound.
No kernel may reach another device: no remote copies, remote signals or barrier semaphores. Data moves between devices by JAX's collectives and lax.ppermute only.
A program may use at most 128 MiB of HBM per device.

v0:
```python
import jax
import jax.numpy as jnp
from jax import lax
from jax.sharding import PartitionSpec as P

H = 12
HD = 64


def norm_rows(values, norm_gain, norm_offset):
    centre = jnp.mean(values, axis=-1, keepdims=True)
    centred = values - centre
    spread = jnp.mean(centred * centred, axis=-1, keepdims=True)
    return centred * lax.rsqrt(spread + 1e-05) * norm_gain + norm_offset


def product(left, right):
    return jnp.dot(left, right, preferred_element_type=jnp.float32)


def along_rows(left, right):
    return lax.dot_general(
        left, right, (((0,), (0,)), ((), ())), preferred_element_type=jnp.float32
    )


def against(left, right):
    return lax.dot_general(
        left, right, (((1,), (1,)), ((), ())), preferred_element_type=jnp.float32
    )


def allowed_mask(begin_row, block_rows, seq_length, length):
    row_ids = begin_row + jnp.arange(block_rows)[:, None]
    col_ids = jnp.arange(seq_length)[None, :]
    return (col_ids <= row_ids) & (col_ids < length)


def shards(
    tokens,
    first_values,
    lengths,
    reuse_index,
    ln1_gain,
    ln1_bias,
    w_query,
    query_bias,
    w_key,
    w_value,
    value_bias,
    w_out,
    out_bias,
    ln2_gain,
    ln2_bias,
    w_up,
    up_bias,
    w_down,
    down_bias,
    cotangent,
):
    local_rows = tokens.shape[0]
    pair_size = lax.axis_size("tensor")
    rank_index = lax.axis_index("tensor")
    seq_length = local_rows * pair_size
    heads_here = w_query.shape[1] // HD
    fresh_here = w_value.shape[1] // HD
    block_rows = min(512, seq_length)
    block_count = seq_length // block_rows
    scale_factor = HD ** (-0.5)
    length = lengths[0]
    positions = rank_index * local_rows + jnp.arange(local_rows)
    valid_rows = (positions < length).astype(jnp.float32)[:, None]
    inputs = tokens.astype(jnp.float32)
    normed_one = norm_rows(inputs, ln1_gain, ln1_bias).astype(jnp.bfloat16)
    picks = lax.dynamic_slice_in_dim(reuse_index, rank_index * fresh_here, fresh_here)
    selector = (picks[:, None] == jnp.arange(H)[None, :]).astype(jnp.bfloat16)
    gathered_one, first_all = (
        lax.all_gather(normed_one, "tensor", axis=0, tiled=True),
        lax.all_gather(first_values, "tensor", axis=0, tiled=True),
    )
    reused = jnp.einsum(
        "jk,skd->sjd",
        selector,
        first_all.reshape(seq_length, H, HD),
        preferred_element_type=jnp.float32,
    ).astype(jnp.bfloat16)
    queries = (product(gathered_one, w_query) + query_bias).astype(jnp.bfloat16)
    key_rows = product(gathered_one, w_key).astype(jnp.bfloat16)
    fresh_rows = (product(gathered_one, w_value) + value_bias).astype(jnp.bfloat16)
    value_heads = jnp.stack(
        [fresh_rows.reshape(seq_length, fresh_here, HD), reused], axis=2
    ).reshape(seq_length, heads_here, HD)
    query_heads = queries.reshape(seq_length, heads_here, HD)
    key_heads = key_rows.reshape(seq_length, heads_here, HD)
    block_starts = jnp.arange(block_count) * block_rows

    def attend_block(begin_row):
        query_block = lax.dynamic_slice_in_dim(query_heads, begin_row, block_rows, 0)
        scores = (
            jnp.einsum("qhd,khd->hqk", query_block, key_heads, preferred_element_type=jnp.float32)
            * scale_factor
        )
        scores = jnp.where(
            allowed_mask(begin_row, block_rows, seq_length, length)[None], scores, -1e30
        )
        highest = jnp.max(scores, axis=-1, keepdims=True)
        weights = jnp.exp(scores - highest)
        totals = jnp.sum(weights, axis=-1, keepdims=True)
        chances = (weights / totals).astype(jnp.bfloat16)
        mixture = jnp.einsum(
            "hqk,khd->qhd", chances, value_heads, preferred_element_type=jnp.float32
        )
        return (mixture, (highest + jnp.log(totals))[..., 0])

    mixtures, log_totals = lax.map(attend_block, block_starts)
    heads_out = mixtures.reshape(seq_length, heads_here * HD).astype(jnp.bfloat16)
    attention = lax.psum_scatter(
        product(heads_out, w_out).astype(jnp.bfloat16), "tensor", scatter_dimension=0, tiled=True
    ).astype(jnp.float32)
    middle = inputs + attention + out_bias
    normed_two = norm_rows(middle, ln2_gain, ln2_bias).astype(jnp.bfloat16)
    gathered_two = lax.all_gather(normed_two, "tensor", axis=0, tiled=True)
    hidden = product(gathered_two, w_up) + up_bias
    active = jax.nn.gelu(hidden).astype(jnp.bfloat16)
    branch = lax.psum_scatter(
        product(active, w_down).astype(jnp.bfloat16), "tensor", scatter_dimension=0, tiled=True
    ).astype(jnp.float32)
    result = ((middle + branch + down_bias) * valid_rows).astype(jnp.bfloat16)
    out_grad = cotangent.astype(jnp.float32) * valid_rows
    down_bias_grad = jnp.sum(out_grad, axis=0)
    branch_grad = lax.all_gather(out_grad.astype(jnp.bfloat16), "tensor", axis=0, tiled=True)
    w_down_grad = along_rows(active, branch_grad)
    active_grad = against(branch_grad, w_down)
    _, gelu_back = jax.vjp(jax.nn.gelu, hidden)
    hidden_grad = gelu_back(active_grad)[0].astype(jnp.bfloat16)
    up_bias_grad = jnp.sum(hidden_grad.astype(jnp.float32), axis=0)
    w_up_grad = along_rows(gathered_two, hidden_grad)
    normed_two_grad = lax.psum_scatter(
        against(hidden_grad, w_up).astype(jnp.bfloat16), "tensor", scatter_dimension=0, tiled=True
    ).astype(jnp.float32)
    _, norm_two_back = jax.vjp(norm_rows, middle, ln2_gain, ln2_bias)
    middle_part, ln2_gain_grad, ln2_bias_grad = norm_two_back(normed_two_grad)
    middle_grad = out_grad + middle_part
    out_bias_grad = jnp.sum(middle_grad, axis=0)
    attention_grad = lax.all_gather(middle_grad.astype(jnp.bfloat16), "tensor", axis=0, tiled=True)
    w_out_grad = along_rows(heads_out, attention_grad)
    heads_grad = (
        against(attention_grad, w_out).astype(jnp.bfloat16).reshape(seq_length, heads_here, HD)
    )

    def back_block(carry, block_input):
        key_grad, value_grad = carry
        begin_row, log_block = block_input
        query_block = lax.dynamic_slice_in_dim(query_heads, begin_row, block_rows, 0)
        grad_block = lax.dynamic_slice_in_dim(heads_grad, begin_row, block_rows, 0)
        scores = (
            jnp.einsum("qhd,khd->hqk", query_block, key_heads, preferred_element_type=jnp.float32)
            * scale_factor
        )
        scores = jnp.where(
            allowed_mask(begin_row, block_rows, seq_length, length)[None], scores, -1e30
        )
        chances = jnp.exp(scores - log_block[..., None])
        value_grad = value_grad + jnp.einsum(
            "hqk,qhd->khd",
            chances.astype(jnp.bfloat16),
            grad_block,
            preferred_element_type=jnp.float32,
        )
        chance_grad = jnp.einsum(
            "qhd,khd->hqk", grad_block, value_heads, preferred_element_type=jnp.float32
        )
        inner = jnp.sum(chances * chance_grad, axis=-1, keepdims=True)
        score_grad = (chances * (chance_grad - inner)).astype(jnp.bfloat16)
        query_grad = (
            jnp.einsum("hqk,khd->qhd", score_grad, key_heads, preferred_element_type=jnp.float32)
            * scale_factor
        )
        key_grad = (
            key_grad
            + jnp.einsum(
                "hqk,qhd->khd", score_grad, query_block, preferred_element_type=jnp.float32
            )
            * scale_factor
        )
        return ((key_grad, value_grad), query_grad)

    zeros = jnp.zeros((seq_length, heads_here, HD), jnp.float32)
    (key_grad, value_grad), query_grads = lax.scan(
        back_block, (zeros, zeros), (block_starts, log_totals)
    )
    query_grad = query_grads.reshape(seq_length, heads_here * HD).astype(jnp.bfloat16)
    key_flat = key_grad.reshape(seq_length, heads_here * HD).astype(jnp.bfloat16)
    split_values = value_grad.reshape(seq_length, fresh_here, 2, HD)
    fresh_grad = split_values[:, :, 0].reshape(seq_length, fresh_here * HD).astype(jnp.bfloat16)
    w_query_grad = along_rows(gathered_one, query_grad)
    query_bias_grad = jnp.sum(query_grad.astype(jnp.float32), axis=0)
    w_key_grad = along_rows(gathered_one, key_flat)
    w_value_grad = along_rows(gathered_one, fresh_grad)
    value_bias_grad = jnp.sum(fresh_grad.astype(jnp.float32), axis=0)
    normed_one_part = (
        against(query_grad, w_query) + against(key_flat, w_key) + against(fresh_grad, w_value)
    )
    first_part = jnp.einsum(
        "sjd,jk->skd",
        split_values[:, :, 1],
        selector.astype(jnp.float32),
        precision=lax.Precision.HIGHEST,
    ).reshape(seq_length, H * HD)
    normed_one_grad, first_values_grad = (
        lax.psum_scatter(
            normed_one_part.astype(jnp.bfloat16), "tensor", scatter_dimension=0, tiled=True
        ).astype(jnp.float32),
        lax.psum_scatter(
            first_part.astype(jnp.bfloat16), "tensor", scatter_dimension=0, tiled=True
        ).astype(jnp.float32),
    )
    _, norm_one_back = jax.vjp(norm_rows, inputs, ln1_gain, ln1_bias)
    input_part, ln1_gain_grad, ln1_bias_grad = norm_one_back(normed_one_grad)
    tokens_grad = middle_grad + input_part
    (
        w_query_grad,
        query_bias_grad,
        w_key_grad,
        w_value_grad,
        value_bias_grad,
        w_out_grad,
        w_up_grad,
        up_bias_grad,
        w_down_grad,
    ) = lax.psum(
        (
            w_query_grad,
            query_bias_grad,
            w_key_grad,
            w_value_grad,
            value_bias_grad,
            w_out_grad,
            w_up_grad,
            up_bias_grad,
            w_down_grad,
        ),
        "dp",
    )
    ln1_gain_grad, ln1_bias_grad, out_bias_grad, ln2_gain_grad, ln2_bias_grad, down_bias_grad = (
        lax.psum(
            (
                ln1_gain_grad,
                ln1_bias_grad,
                out_bias_grad,
                ln2_gain_grad,
                ln2_bias_grad,
                down_bias_grad,
            ),
            ("dp", "tensor"),
        )
    )
    return (
        result,
        tokens_grad,
        first_values_grad,
        ln1_gain_grad,
        ln1_bias_grad,
        w_query_grad,
        query_bias_grad,
        w_key_grad,
        w_value_grad,
        value_bias_grad,
        w_out_grad,
        out_bias_grad,
        ln2_gain_grad,
        ln2_bias_grad,
        w_up_grad,
        up_bias_grad,
        w_down_grad,
        down_bias_grad,
    )


def solution(mesh):
    in_specs = (
        P(("dp", "tensor"), None),
        P(("dp", "tensor"), None),
        P("dp"),
        P(),
        P(),
        P(),
        P(None, "tensor"),
        P("tensor"),
        P(None, "tensor"),
        P(None, "tensor"),
        P("tensor"),
        P("tensor", None),
        P(),
        P(),
        P(),
        P(None, "tensor"),
        P("tensor"),
        P("tensor", None),
        P(),
        P(("dp", "tensor"), None),
    )
    out_specs = (
        P(("dp", "tensor"), None),
        P(("dp", "tensor"), None),
        P(("dp", "tensor"), None),
        P(),
        P(),
        P(None, "tensor"),
        P("tensor"),
        P(None, "tensor"),
        P(None, "tensor"),
        P("tensor"),
        P("tensor", None),
        P(),
        P(),
        P(),
        P(None, "tensor"),
        P("tensor"),
        P("tensor", None),
        P(),
    )
    return jax.shard_map(shards, mesh=mesh, in_specs=in_specs, out_specs=out_specs, check_vma=False)
```

profile of v0, /device:TPU:0, one launch (start us, length us, event | category | flops | bytes accessed | tf_op | source)
XLA Modules:
  0.0 713.2 jit_solution(3048459015327138377)
XLA Ops:
  15.3 27.5 %all-gather.6.cloned.1.call-done = bf16[1024,768]{1,0:T(8,128)(2,1)} async-done(((bf16[512,768]{1,0:T(8,128)(2,1)}), bf16[1024,768]{1,0:T(8,128)(2,1)}) %all-gather.6.cloned.1.call-update) | async-done | bytes 1572880 | tf_op jit(solution)/shard_map/all_gather | solution.py:78
  45.2 26.9 %all-gather.8.cloned.1.call-done = bf16[1024,768]{0,1:T(8,128)(2,1)} async-done(((bf16[512,768]{0,1:T(8,128)(2,1)}), bf16[1024,768]{0,1:T(8,128)(2,1)}) %all-gather.8.cloned.1.call-update) | async-done | bytes 1572880 | tf_op jit(solution)/shard_map/all_gather | solution.py:79
  80.3 34.3 %while.27 = (s32[]{:T(128)}, bf16[2,512,6,64]{1,3,2,0:T(8,128)(2,1)}, f32[2,6,512]{2,1,0:T(8,128)S(1)}, s32[2]{0:T(128)S(1)}, s32[]{:T(128)}, /*index=5*/bf16[10...) while((s32[]{:T(128)}, ...), condition=%wide.region_5.6_spmd, body=%wide.region_2.5_spmd.sunk | while | flops 844102144 | bytes 52160780 | solution.py:115
  84.5 3.9 fusion.153
  88.5 3.6 fusion.154
  92.1 4.4 fusion.155
  101.7 3.9 fusion.153
  105.6 3.6 fusion.154
  109.3 4.4 fusion.155
  120.3 25.8 %reduce-scatter.6.cloned.1.call-done = bf16[512,768]{1,0:T(8,128)(2,1)} async-done(((bf16[1024,768]{1,0:T(8,128)(2,1)}), bf16[512,768]{1,0:T(8,128)(2,1)}) %reduce-scatter.6.cloned.1.call-update) | async-done | bytes 786448 | tf_op jit(solution)/shard_map/reduce_scatter | solution.py:117
  152.8 24.4 %all-gather.10.cloned.1.call-done = bf16[1024,768]{1,0:T(8,128)(2,1)} async-done(((bf16[512,768]{1,0:T(8,128)(2,1)}), bf16[1024,768]{1,0:T(8,128)(2,1)}) %all-gather.10.cloned.1.call-update) | async-done | bytes 1572880 | tf_op jit(solution)/shard_map/all_gather | solution.py:122
  177.2 7.4 %fusion.80 = f32[1024,1536]{1,0:T(8,128)} fusion(bf16[1024,768]{1,0:T(8,128)(2,1)} %all-gather.10.cloned.1.call-done, bf16[768,1536]{1,0:T(8,128)(2,1)} %param.39), kind=kOutput, calls=%fused_computation.133 | convolution fusion | flops 2415919104 | bytes 10223616 | tf_op jit(solution)/shard_map/dot_general | solution.py:18
  184.5 21.9 %all-gather.12.cloned.1.call-done = bf16[1024,768]{1,0:T(8,128)(2,1)} async-done(((bf16[512,768]{1,0:T(8,128)(2,1)}), bf16[1024,768]{1,0:T(8,128)(2,1)}) %all-gather.12.cloned.1.call-update) | async-done | bytes 1572880 | tf_op jit(solution)/shard_map/all_gather | solution.py:131
  206.5 10.6 %convert_reduce_fusion = (f32[1536]{0:T(1024)}, bf16[1024,1536]{1,0:T(8,128)(2,1)S(1)}, bf16[1024,1536]{1,0:T(8,128)(2,1)}) fusion(f32[1024,1536]{1,0:T(8,128)} %fusion.80, f32[1536]{0:T(1024)S(1)} %copy-done.63, bf16[1024,768]{1,0:T(8,128)(2,1)} %all-gather.12.cloned.1.call-done, bf16[1536,768]{1,0:T(8,128)(2,1)S(1)} %copy-done), kind=kOutput, calls=%fused_computation.55 | convolution fusion | flops 2455239168 | bytes 16527360 | tf_op jit(solution)/shard_map/dot_general | solution.py:28
  218.7 3.7 convolution_convert_fusion.1
  222.5 5.6 convolution_convert_fusion.2
  228.2 20.4 %reduce-scatter.10.cloned.1.call-done = bf16[512,768]{1,0:T(8,128)(2,1)} async-done(((bf16[1024,768]{1,0:T(8,128)(2,1)}), bf16[512,768]{1,0:T(8,128)(2,1)}) %reduce-scatter.10.cloned.1.call-update) | async-done | bytes 786448 | tf_op jit(solution)/shard_map/reduce_scatter | solution.py:138
  252.8 24.8 %reduce-scatter.8.cloned.1.call-done = bf16[512,768]{1,0:T(8,128)(2,1)} async-done(((bf16[1024,768]{1,0:T(8,128)(2,1)}), bf16[512,768]{1,0:T(8,128)(2,1)}) %reduce-scatter.8.cloned.1.call-update) | async-done | bytes 786448 | tf_op jit(solution)/shard_map/reduce_scatter | solution.py:125
  277.6 3.8 fusion.79
  283.6 27.3 %all-gather.14.cloned.1.call-done = bf16[1024,768]{1,0:T(8,128)(2,1)} async-done(((bf16[512,768]{1,0:T(8,128)(2,1)}), bf16[1024,768]{1,0:T(8,128)(2,1)}) %all-gather.14.cloned.1.call-update) | async-done | bytes 1572880 | tf_op jit(solution)/shard_map/all_gather | solution.py:145
  314.9 58.1 %while.28 = (s32[]{:T(128)}, f32[1024,6,64]{0,2,1:T(8,128)S(1)}, f32[1024,6,64]{0,2,1:T(8,128)}, bf16[2,512,6,64]{1,3,2,0:T(8,128)(2,1)}, s32[2]{0:T(128)S(1)}, ...) while((s32[]{:T(128)}, f32[1024,6,64]{0,2,1:T(8,128)S(1)}, ...), condition=%wide.region_15.16_spmd.clone, body=%wide.region_13.15_spmd.clone.sunk | while | flops 2063661568 | bytes 135891392 | solution.py:189
  322.6 3.5 bitcast_add_fusion.5
  326.1 7.5 %multiply_reduce_fusion.3 = (f32[6,512]{1,0:T(8,128)S(1)}, f32[6,512,1024]{2,1,0:T(8,128)}) fusion(f32[6,512,1024]{2,1,0:T(8,128)S(1)} %fusion.165, f32[6,512]{1,0:T(8,128)S(1)} %dynamic-slice_bitcast_fusion.2, pred[512,1024]{1,0:T(8,128)(4,1)S(1)} %fusion.166, bf16[1024,6,64]{0,2,1:T(8,128)(2,1)S(1)} %copy-done.8, ...), kind=kOutput, calls=%fused_computation.19.clone.1 | convolution fusion | flops 418378752 | bytes 26898436 | tf_op jit(solution)/shard_map/while/body/eval_jaxpr/qhd,khd->hqk/dot_general | solution.py:170
  333.6 6.9 multiply_convert_fusion.4
  351.5 3.5 bitcast_add_fusion.5
  355.0 7.5 %multiply_reduce_fusion.3 = (f32[6,512]{1,0:T(8,128)S(1)}, f32[6,512,1024]{2,1,0:T(8,128)}) fusion(f32[6,512,1024]{2,1,0:T(8,128)S(1)} %fusion.165, f32[6,512]{1,0:T(8,128)S(1)} %dynamic-slice_bitcast_fusion.2, pred[512,1024]{1,0:T(8,128)(4,1)S(1)} %fusion.166, bf16[1024,6,64]{0,2,1:T(8,128)(2,1)S(1)} %copy-done.8, ...), kind=kOutput, calls=%fused_computation.19.clone.1 | convolution fusion | flops 418378752 | bytes 26898436 | tf_op jit(solution)/shard_map/while/body/eval_jaxpr/qhd,khd->hqk/dot_general | solution.py:170
  362.5 6.9 multiply_convert_fusion.4
  385.5 7.4 %fusion.86 = f32[768,1536]{1,0:T(8,128)} fusion(bf16[1024,768]{1,0:T(8,128)(2,1)} %all-gather.10.cloned.1.call-done, bf16[1024,1536]{1,0:T(8,128)(2,1)} %copy-done.22), kind=kOutput, calls=%fused_computation.139 | convolution fusion | flops 2415919104 | bytes 9437184 | tf_op jit(solution)/shard_map/dot_general | solution.py:22
  392.9 4.6 fusion.87
  406.0 62.7 %all-reduce.1 = (f32[384]{0:T(512)}, f32[192]{0:T(256)}, f32[1536]{0:T(1024)}) all-reduce(f32[384]{0:T(512)S(1)} %reduce_sum.193, f32[192]{0:T(256)S(1)} %reduce_sum.198, f32[1536]{0:T(1024)S(1)} %copy-done.52), channel_id=1, replica_groups=mesh['dp'=16,'tensor'=2] {'dp'}, use_global_device_ids=true, to_apply=%region_26.27 | all-reduce | flops 2112 | bytes 16896 | tf_op jit(solution)/shard_map/psum | solution.py:231
  475.4 39.0 %all-reduce = (f32[768]{0:T(1024)}, f32[768]{0:T(1024)}, f32[768]{0:T(1024)}, f32[768]{0:T(1024)}, f32[768]{0:T(1024)}, /*index=5*/f32[768]{0:T(1024)}) all-reduce(f32[768]{0:T(1024)S(1)} %get-tuple-element.181, f32[768]{0:T(1024)S(1)} %get-tuple-element.185, ...), channel_id=1, replica_groups=mesh['dp'=16,'tensor'=2] {'dp','tensor'}, use_global_device_ids=true, to_apply=%region_21.22 | all-reduce | flops 4608 | bytes 36864 | tf_op jit(solution)/shard_map/psum | solution.py:246
  516.1 178.3 %all-reduce.5.cloned.1.call-done = (f32[768,384]{1,0:T(8,128)}, f32[768,384]{1,0:T(8,128)}, f32[768,192]{0,1:T(8,128)}, f32[384,768]{1,0:T(8,128)}, f32[768,1536]{1,0:T(8,128)}, /*index=5*/f32[1536,768]{1,0:T(8,128)}) async-done(((f32[768,384]{1,0:T(8,128)}, f32[768,384]{1,0:T(8,128)}, f32[768,192]{0,1:T(8,128)}, f32[384,768]{1,0:T(8,128)}, f32[768,1536]{1,0:T(8,128)}, /*index=5*/f32[1536,768]{1,0:T(8,128)}), ...) | async-done | bytes 13565968 | tf_op jit(solution)/shard_map/psum | solution.py:231
  (275 shorter events, 107.3 us)
Async XLA Ops:
  7.2 199.3 %copy-start = (bf16[1536,768]{1,0:T(8,128)(2,1)S(1)}, bf16[1536,768]{1,0:T(8,128)(2,1)}, u32[]{:S(2)}) copy-start(bf16[1536,768]{1,0:T(8,128)(2,1)} %param.41) | copy-start | bytes 7077892
  7.2 35.5 %all-gather.6.cloned.1.call-start = ((), (), s32[]{:S(2)}) async-start(), calls=%async_computation.5 | async-start | bytes 2359296 | tf_op jit(solution)/shard_map/all_gather | solution.py:78
  12.7 30.1 %copy-start.36 = (bf16[768,192]{0,1:T(8,128)(2,1)S(1)}, bf16[768,192]{0,1:T(8,128)(2,1)}, u32[]{:S(2)}) copy-start(bf16[768,192]{0,1:T(8,128)(2,1)} %param.33) | copy-start | bytes 884740
  12.7 30.1 %copy-start.65 = (f32[192]{0:T(256)S(1)}, f32[192]{0:T(256)}, u32[]{:S(2)}) copy-start(f32[192]{0:T(256)} %param.34) | copy-start | bytes 2308
  12.7 59.4 %all-gather.8.cloned.1.call-start = ((), (), s32[]{:S(2)}) async-start(), calls=%async_computation.6 | async-start | bytes 2359296 | tf_op jit(solution)/shard_map/all_gather | solution.py:79
  15.1 131.0 %reduce-scatter.6.cloned.1.call-start = ((), (), s32[]{:S(2)}) async-start(), calls=%async_computation.7 | async-start | bytes 2359296 | tf_op jit(solution)/shard_map/reduce_scatter | solution.py:117
  15.3 56.9 %copy-start.56 = (s32[3]{0:T(128)}, s32[3]{0:T(128)S(1)}, u32[]{:S(2)}) copy-start(s32[3]{0:T(128)S(1)} %dynamic_slice.23) | copy-start | bytes 40
  117.7 28.4 %copy-start.38 = (f32[768]{0:T(1024)S(1)}, f32[768]{0:T(1024)}, u32[]{:S(2)}) copy-start(f32[768]{0:T(1024)} %param.36) | copy-start | bytes 9220
  119.9 28.6 %copy-start.41 = (f32[768]{0:T(1024)S(1)}, f32[768]{0:T(1024)}, u32[]{:S(2)}) copy-start(f32[768]{0:T(1024)} %param.37) | copy-start | bytes 9220
  119.9 28.6 %copy-start.54 = (f32[768]{0:T(1024)S(1)}, f32[768]{0:T(1024)}, u32[]{:S(2)}) copy-start(f32[768]{0:T(1024)} %param.38) | copy-start | bytes 9220
  119.9 57.3 %all-gather.10.cloned.1.call-start = ((), (), s32[]{:S(2)}) async-start(), calls=%async_computation.8 | async-start | bytes 2359296 | tf_op jit(solution)/shard_map/all_gather | solution.py:122
  149.8 56.7 %all-gather.12.cloned.1.call-start = ((), (), s32[]{:S(2)}) async-start(), calls=%async_computation.10 | async-start | bytes 2359296 | tf_op jit(solution)/shard_map/all_gather | solution.py:131
  152.7 53.7 %copy-start.63 = (f32[1536]{0:T(1024)S(1)}, f32[1536]{0:T(1024)}, u32[]{:S(2)}) copy-start(f32[1536]{0:T(1024)} %param.40) | copy-start | bytes 18436
  152.7 95.9 %reduce-scatter.10.cloned.1.call-start = ((), (), s32[]{:S(2)}) async-start(), calls=%async_computation.11 | async-start | bytes 2359296 | tf_op jit(solution)/shard_map/reduce_scatter | solution.py:138
  206.4 12.3 %copy-start.58 = (bf16[768,1536]{1,0:T(8,128)(2,1)S(1)}, bf16[768,1536]{1,0:T(8,128)(2,1)}, u32[]{:S(2)}) copy-start(bf16[768,1536]{1,0:T(8,128)(2,1)} %param.39) | copy-start | bytes 7077892
  222.5 55.1 %reduce-scatter.8.cloned.1.call-start = ((), (), s32[]{:S(2)}) async-start(), calls=%async_computation.9 | async-start | bytes 2359296 | tf_op jit(solution)/shard_map/reduce_scatter | solution.py:125
  228.2 20.5 %copy-start.4 = (bf16[512,768]{1,0:T(8,128)(2,1)S(1)}, bf16[512,768]{1,0:T(8,128)(2,1)}, u32[]{:S(2)}) copy-start(bf16[512,768]{1,0:T(8,128)(2,1)} %param.24) | copy-start | bytes 2359300
  228.2 20.5 %copy-start.10 = (bf16[512,768]{1,0:T(8,128)(2,1)S(1)}, bf16[512,768]{1,0:T(8,128)(2,1)}, u32[]{:S(2)}) copy-start(bf16[512,768]{1,0:T(8,128)(2,1)} %reduce-scatter.6.cloned.1.call-done) | copy-start | bytes 2359300
  228.2 82.7 %all-gather.14.cloned.1.call-start = ((), (), s32[]{:S(2)}) async-start(), calls=%async_computation.12 | async-start | bytes 2359296 | tf_op jit(solution)/shard_map/all_gather | solution.py:145
  251.2 26.4 %copy-start.55 = (f32[768]{0:T(1024)S(1)}, f32[768]{0:T(1024)}, u32[]{:S(2)}) copy-start(f32[768]{0:T(1024)} %param.42) | copy-start | bytes 9220
  282.5 28.4 %copy-start.62 = (bf16[384,768]{1,0:T(8,128)(2,1)S(1)}, bf16[384,768]{1,0:T(8,128)(2,1)}, u32[]{:S(2)}) copy-start(bf16[384,768]{1,0:T(8,128)(2,1)} %param.35) | copy-start | bytes 1769476
  283.5 185.2 %reduce-scatter.14.cloned.1.call-start = ((), (), s32[]{:S(2)}) async-start(), calls=%async_computation.14 | async-start | bytes 2359296 | tf_op jit(solution)/shard_map/reduce_scatter | solution.py:214
  326.1 7.5 %copy-start.28 = (f32[1024,6,64]{0,2,1:T(8,128)}, f32[1024,6,64]{0,2,1:T(8,128)S(1)}, u32[]{:S(2)}) copy-start(f32[1024,6,64]{0,2,1:T(8,128)S(1)} %bitcast_add_fusion.5) | copy-start | bytes 4718596 | tf_op jit(solution)/shard_map/while
  355.0 7.5 %copy-start.28 = (f32[1024,6,64]{0,2,1:T(8,128)}, f32[1024,6,64]{0,2,1:T(8,128)S(1)}, u32[]{:S(2)}) copy-start(f32[1024,6,64]{0,2,1:T(8,128)S(1)} %bitcast_add_fusion.5) | copy-start | bytes 4718596 | tf_op jit(solution)/shard_map/while
  379.4 91.9 %reduce-scatter.12.cloned.1.call-start = ((), (), s32[]{:S(2)}) async-start(), calls=%async_computation.13 | async-start | bytes 2359296 | tf_op jit(solution)/shard_map/reduce_scatter | solution.py:211
  385.5 308.9 %all-reduce.5.cloned.1.call-start = ((), (), s32[]{:S(2)}) async-start(), calls=%async_computation.15 | async-start | bytes 27131904 | tf_op jit(solution)/shard_map/psum | solution.py:231
  385.5 7.4 %copy-start.59 = (bf16[1024,768]{1,0:T(8,128)(2,1)S(1)}, bf16[1024,768]{1,0:T(8,128)(2,1)}, u32[]{:S(2)}) copy-start(bf16[1024,768]{1,0:T(8,128)(2,1)} %all-gather.12.cloned.1.call-done) | copy-start | bytes 4718596
  405.4 65.9 %copy-start.5 = (bf16[512,768]{1,0:T(8,128)(2,1)S(1)}, bf16[512,768]{1,0:T(8,128)(2,1)}, u32[]{:S(2)}) copy-start(bf16[512,768]{1,0:T(8,128)(2,1)} %param.24) | copy-start | bytes 2359300
  405.4 65.9 %copy-start.40 = (f32[512]{0:T(512)S(1)}, f32[512]{0:T(512)}, u32[]{:S(2)}) copy-start(f32[512]{0:T(512)} %copy-done.39) | copy-start | bytes 6148
  405.4 65.9 %copy-start.43 = (f32[768]{0:T(1024)S(1)}, f32[768]{0:T(1024)}, u32[]{:S(2)}) copy-start(f32[768]{0:T(1024)} %param.28) | copy-start | bytes 9220
  471.3 43.1 %copy-start.12 = (f32[512,768]{1,0:T(8,128)S(1)}, f32[512,768]{1,0:T(8,128)}, u32[]{:S(2)}) copy-start(f32[512,768]{1,0:T(8,128)} %copy-done.11) | copy-start | bytes 4718596
  471.3 43.1 %copy-start.17 = (bf16[512,768]{1,0:T(8,128)(2,1)S(1)}, bf16[512,768]{1,0:T(8,128)(2,1)}, u32[]{:S(2)}) copy-start(bf16[512,768]{1,0:T(8,128)(2,1)} %reduce-scatter.12.cloned.1.call-done) | copy-start | bytes 2359300
  (59 other events, 164.9 us)
Sparse Core Ops, SparseCore 0:
  12.8 29.8 all-gather.5
  44.9 27.1 all-gather.7
  120.0 26.0 reduce-scatter.5
  149.9 27.2 all-gather.9
  179.2 27.2 all-gather.11
  222.6 26.0 reduce-scatter.9
  251.5 26.0 reduce-scatter.7
  283.6 27.2 all-gather.13
  379.5 26.0 reduce-scatter.13
  407.7 26.0 reduce-scatter.11
  441.7 252.6 all-reduce.4
where the time goes:
time: 724 us; the launch traced here: 713 us
  waiting for transfers between devices  378 us (52%)
  matrix products  117 us (16%)
  blocking collectives  102 us (14%)
  other arithmetic  55.1 us (8%)
  local copies, waits for them, and re-layouts  36.8 us (5%)
  between operations  15.5 us (2%)
  loops' own time  8.43 us (1%)
    psum x1, waiting for transfers between devices, shards(): lax.psum((w_query_grad, query_bias_grad, w_key_grad, w_value_grad, value_...  178 us
    psum x1, blocking collectives, shards(): lax.psum((w_query_grad, query_bias_grad, w_key_grad, w_value_grad, value_...  62.7 us
    psum x1, blocking collectives, shards(): lax.psum((ln1_gain_grad, ln1_bias_grad, out_bias_grad, ln2_gain_grad, ln2...  39 us
    all_gather x1, waiting for transfers between devices, shards(): lax.all_gather(normed_one, 'tensor', axis=0, tiled=True)  27.5 us
    all_gather x1, waiting for transfers between devices, shards(): lax.all_gather(middle_grad.astype(jnp.bfloat16), 'tensor', axis=0, tiled=...  27.3 us
    all_gather x1, waiting for transfers between devices, shards(): lax.all_gather(first_values, 'tensor', axis=0, tiled=True)  26.9 us
    reduce_scatter x1, waiting for transfers between devices, shards(): lax.psum_scatter(product(heads_out, w_out).astype(jnp.bfloat16), 'tensor'...  25.8 us
    reduce_scatter x1, waiting for transfers between devices, shards(): lax.psum_scatter(product(active, w_down).astype(jnp.bfloat16), 'tensor',...  24.8 us
  transfers between devices with their start and end apart: 11, of which 9 were waited for; matrix products, arithmetic and copies ran while one was open for 8% of the time, Pallas kernels for 0%

commit v1 on v0

v1 whole, which is shorter than its diff:
```python
from functools import partial

import jax
import jax.numpy as jnp
from jax import lax
from jax.experimental import pallas as pl
from jax.experimental.pallas import tpu as pltpu
from jax.sharding import PartitionSpec as P

H = 12
HD = 64
PARTS = 2
HINT = pl.CostEstimate(flops=1 << 20, bytes_accessed=1 << 16, transcendentals=0)


def norm_rows(values, norm_gain, norm_offset):
    centre = jnp.mean(values, axis=-1, keepdims=True)
    centred = values - centre
    spread = jnp.mean(centred * centred, axis=-1, keepdims=True)
    return centred * lax.rsqrt(spread + 1e-05) * norm_gain + norm_offset


def across(values):
    return lax.ppermute(values, "tensor", [(0, 1), (1, 0)])


def flip(values, bit):
    return lax.ppermute(values, "dp", [(d, d ^ bit) for d in range(lax.axis_size("dp"))])


def halves(values, which):
    half = values.shape[0] // 2
    return (
        lax.dynamic_slice_in_dim(values, which * half, half, 0),
        lax.dynamic_slice_in_dim(values, (1 - which) * half, half, 0),
    )


def join(own, other, which):
    return jnp.concatenate(
        [jnp.where(which == 0, own, other), jnp.where(which == 0, other, own)], axis=0
    )


def slabs(values, which):
    half = values.shape[1] // 2
    return (
        lax.dynamic_slice_in_dim(values, which * half, half, 1),
        lax.dynamic_slice_in_dim(values, (1 - which) * half, half, 1),
    )


def dp_bits():
    return [1 << k for k in range(lax.axis_size("dp").bit_length() - 1)]


class Chain:
    def __init__(self, values, place):
        self.values, self.place = values, place
        self.steps = [("halve", bit) for bit in dp_bits()]
        self.steps += [("double", bit) for bit in reversed(dp_bits())]

    def step(self):
        if not self.steps:
            return
        kind, bit = self.steps.pop(0)
        which = (self.place // bit) % 2
        if kind == "halve":
            keep, send = halves(self.values, which)
            self.values = (
                keep.astype(jnp.float32) + flip(send, bit).astype(jnp.float32)
            ).astype(jnp.bfloat16)
        else:
            self.values = join(self.values, flip(self.values, bit), which)

    def finish(self):
        while self.steps:
            self.step()
        return self.values


def advance(chains, counts):
    for chain, count in zip(chains, counts):
        for _ in range(count):
            chain.step()


def hold(chains, *values):
    flat = lax.optimization_barrier(tuple(c.values for c in chains) + values)
    for chain, held in zip(chains, flat):
        chain.values = held
    return flat[len(chains) :] if len(values) != 1 else flat[-1]


def after(values, *found):
    return lax.optimization_barrier((values, found))[0]


def reduce_small(values):
    for bit in dp_bits():
        values = values + flip(values, bit)
    return values


NT = (((1,), (1,)), ((), ()))
TN = (((0,), (0,)), ((), ()))
NN = (((1,), (0,)), ((), ()))
BLOCK = 256
VMEM_BYTES = 48 * 1024 * 1024


def dot(left, right, dims):
    return lax.dot_general(left, right, dims, preferred_element_type=jnp.float32)


def score_parts(k_ref, query, begin, length, sure):
    parts = []
    for first, last in ((0, begin), (begin, begin + BLOCK)):
        if last > first:
            part = dot(k_ref[first:last, :], query, NT)
            keys = lax.broadcasted_iota(jnp.int32, part.shape, 0) + first
            if first == begin:
                queries = lax.broadcasted_iota(jnp.int32, part.shape, 1) + begin
                part = jnp.where((keys <= queries) & (keys < length), part, -1e30)
            elif last > sure:
                part = jnp.where(keys < length, part, -1e30)
            parts.append((first, last, part))
    return parts


def attend_kernel(sure, length_ref, q_ref, k_ref, v_ref, out_ref, lse_ref):
    length = length_ref[0]
    rows = q_ref.shape[0]
    for begin in range(0, rows, BLOCK):
        query = q_ref[begin : begin + BLOCK, :] * HD ** (-0.5)
        lane = lax.broadcasted_iota(jnp.int32, query.shape, 1)
        mixed = []
        for side in range(2):
            mine = (lane < HD) if side == 0 else (lane >= HD)
            parts = score_parts(k_ref, jnp.where(mine, query, 0).astype(query.dtype), begin, length, sure)
            highest = None
            for _, _, part in parts:
                top = jnp.max(part, axis=0, keepdims=True)
                highest = top if highest is None else jnp.maximum(highest, top)
            total, mix = 0.0, 0.0
            for first, last, part in parts:
                weights = jnp.exp(part - highest)
                total = total + jnp.sum(weights, axis=0, keepdims=True)
                mix = mix + dot(v_ref[first:last, :], weights.astype(jnp.bfloat16), TN)
            mixed.append(mix * (1.0 / total))
            lse_ref[0, side : side + 1, begin : begin + BLOCK] = highest + jnp.log(total)
        row = lax.broadcasted_iota(jnp.int32, mixed[0].shape, 0)
        both = jnp.where(row < HD, mixed[0], mixed[1])
        out_ref[begin : begin + BLOCK, :] = both.T.astype(jnp.bfloat16)


def attend(length, queries, keys, values, sure):
    rows, width = queries.shape
    pairs = width // (2 * HD)
    column = pl.BlockSpec((rows, 2 * HD), lambda p, *_: (0, p))
    return pl.pallas_call(
        partial(attend_kernel, sure),
        grid_spec=pltpu.PrefetchScalarGridSpec(
            num_scalar_prefetch=1,
            grid=(pairs,),
            in_specs=[column] * 3,
            out_specs=[column, pl.BlockSpec((1, 2, rows), lambda p, *_: (p, 0, 0))],
        ),
        out_shape=[
            jax.ShapeDtypeStruct((rows, width), jnp.bfloat16),
            jax.ShapeDtypeStruct((pairs, 2, rows), jnp.float32),
        ],
        compiler_params=pltpu.CompilerParams(vmem_limit_bytes=VMEM_BYTES),
        cost_estimate=HINT,
    )(length, queries, keys, values)


def attend_back_kernel(
    sure, length_ref, q_ref, k_ref, v_ref, out_ref, lse_ref, grad_ref, dq_ref, dk_ref, dv_ref, dk_sum, dv_sum
):
    length = length_ref[0]
    rows = q_ref.shape[0]
    dk_sum[...] = jnp.zeros_like(dk_sum)
    dv_sum[...] = jnp.zeros_like(dv_sum)
    for begin in range(0, rows, BLOCK):
        block = slice(begin, begin + BLOCK)
        query = q_ref[block, :] * HD ** (-0.5)
        grad = grad_ref[block, :]
        product = (grad.astype(jnp.float32) * out_ref[block, :].astype(jnp.float32)).T
        lane = lax.broadcasted_iota(jnp.int32, query.shape, 1)
        found = []
        for side in range(2):
            mine = (lane < HD) if side == 0 else (lane >= HD)
            own_query = jnp.where(mine, query, 0).astype(query.dtype)
            own_grad = jnp.where(mine, grad, 0).astype(grad.dtype)
            inner = jnp.sum(product[side * HD : (side + 1) * HD, :], axis=0, keepdims=True)
            lse = lse_ref[0, side : side + 1, block]
            query_grad = 0.0
            for first, last, part in score_parts(k_ref, own_query, begin, length, sure):
                chances = jnp.exp(part - lse)
                chance_grad = dot(v_ref[first:last, :], own_grad, NT)
                score_grad = (chances * (chance_grad - inner)).astype(jnp.bfloat16)
                dv_sum[first:last, :] += dot(chances.astype(jnp.bfloat16), own_grad, NN)
                dk_sum[first:last, :] += dot(score_grad, own_query, NN)
                query_grad = query_grad + dot(k_ref[first:last, :], score_grad, TN)
            found.append(query_grad)
        row = lax.broadcasted_iota(jnp.int32, found[0].shape, 0)
        both = jnp.where(row < HD, found[0], found[1]) * HD ** (-0.5)
        dq_ref[block, :] = both.T.astype(jnp.bfloat16)
    dk_ref[...] = dk_sum[...].astype(jnp.bfloat16)
    dv_ref[...] = dv_sum[...].astype(jnp.bfloat16)


def attend_back(length, queries, keys, values, heads_out, lse, heads_grad, sure):
    rows, width = queries.shape
    pairs = width // (2 * HD)
    column = pl.BlockSpec((rows, 2 * HD), lambda p, *_: (0, p))
    lse_spec = pl.BlockSpec((1, 2, rows), lambda p, *_: (p, 0, 0))
    shape = jax.ShapeDtypeStruct((rows, width), jnp.bfloat16)
    return pl.pallas_call(
        partial(attend_back_kernel, sure),
        grid_spec=pltpu.PrefetchScalarGridSpec(
            num_scalar_prefetch=1,
            grid=(pairs,),
            in_specs=[column] * 4 + [lse_spec, column],
            out_specs=[column] * 3,
            scratch_shapes=[pltpu.VMEM((rows, 2 * HD), jnp.float32)] * 2,
        ),
        out_shape=[shape] * 3,
        compiler_params=pltpu.CompilerParams(vmem_limit_bytes=VMEM_BYTES),
        cost_estimate=HINT,
    )(length, queries, keys, values, heads_out, lse, heads_grad)


def gelu_parts(hidden):
    rate = 0.7978845608028654
    square = hidden * hidden
    bend = jnp.tanh(rate * hidden * (1.0 + 0.044715 * square))
    lift = 0.5 * (1.0 + bend)
    slope = lift + 0.5 * hidden * (1.0 - bend * bend) * (rate * (1.0 + 3 * 0.044715 * square))
    return hidden * lift, slope


def feed_kernel(
    normed_ref,
    grad_ref,
    up_ref,
    bias_ref,
    down_ref,
    branch_ref,
    back_ref,
    active_ref,
    hidden_grad_ref,
    bias_grad_ref,
):
    normed, grad = normed_ref[...], grad_ref[...]
    up, down = up_ref[...], down_ref[...]
    active, slope = gelu_parts(dot(normed, up, NN) + bias_ref[...])
    active = active.astype(jnp.bfloat16)
    hidden_grad = (dot(grad, down, NT) * slope).astype(jnp.bfloat16)

    @pl.when(pl.program_id(0) == 0)
    def _():
        branch_ref[...] = jnp.zeros_like(branch_ref)
        back_ref[...] = jnp.zeros_like(back_ref)

    branch_ref[...] += dot(active, down, NN)
    back_ref[...] += dot(hidden_grad, up, NT)
    active_ref[...] = active
    hidden_grad_ref[...] = hidden_grad
    bias_grad_ref[...] = jnp.sum(hidden_grad.astype(jnp.float32), axis=0, keepdims=True)


def feed(normed, grad, w_up, up_bias, w_down):
    rows, width = normed.shape
    hidden = w_down.shape[0]
    tile = BLOCK
    whole = pl.BlockSpec((rows, width), lambda i: (0, 0))
    part = pl.BlockSpec((rows, tile), lambda i: (0, i))
    return pl.pallas_call(
        feed_kernel,
        grid=(hidden // tile,),
        in_specs=[
            whole,
            whole,
            pl.BlockSpec((width, tile), lambda i: (0, i)),
            pl.BlockSpec((1, tile), lambda i: (0, i)),
            pl.BlockSpec((tile, width), lambda i: (i, 0)),
        ],
        out_specs=[whole, whole, part, part, pl.BlockSpec((1, tile), lambda i: (0, i))],
        out_shape=[
            jax.ShapeDtypeStruct((rows, width), jnp.float32),
            jax.ShapeDtypeStruct((rows, width), jnp.float32),
            jax.ShapeDtypeStruct((rows, hidden), jnp.bfloat16),
            jax.ShapeDtypeStruct((rows, hidden), jnp.bfloat16),
            jax.ShapeDtypeStruct((1, hidden), jnp.float32),
        ],
        compiler_params=pltpu.CompilerParams(vmem_limit_bytes=VMEM_BYTES),
        cost_estimate=HINT,
    )(normed, grad, w_up, up_bias[None], w_down)


def feed_weights_kernel(tiles, *refs):
    active_refs, hidden_grad_refs, normed_refs, grad_refs = refs[0:2], refs[2:4], refs[4:6], refs[6:8]
    out_ref = refs[8]
    for k in range(tiles):
        part = slice(k * BLOCK, (k + 1) * BLOCK)
        down = sum(dot(a[:, part], g[...], TN) for a, g in zip(active_refs, grad_refs))
        out_ref[0, part, :] = down.astype(jnp.bfloat16)
        up = sum(dot(n[...], h[:, part], TN) for n, h in zip(normed_refs, hidden_grad_refs))
        out_ref[1, :, part] = up.astype(jnp.bfloat16)


def feed_weights(part, actives, hidden_grads, normeds, grads):
    rows, width = normeds[0].shape
    hidden = actives[0].shape[1] // PARTS
    whole = pl.BlockSpec((rows, width), lambda i: (0, 0))
    column = pl.BlockSpec((rows, hidden), lambda i: (0, part))
    return pl.pallas_call(
        partial(feed_weights_kernel, hidden // BLOCK),
        grid=(1,),
        in_specs=[column] * 4 + [whole] * 4,
        out_specs=pl.BlockSpec((2, hidden, width), lambda i: (0, 0, 0)),
        out_shape=jax.ShapeDtypeStruct((2, hidden, width), jnp.bfloat16),
        compiler_params=pltpu.CompilerParams(vmem_limit_bytes=VMEM_BYTES),
        cost_estimate=HINT,
    )(*actives, *hidden_grads, *normeds, *grads)


def project_kernel(x_ref, w_ref, qb_ref, vb_ref, reused_ref, q_ref, k_ref, v_ref):
    width = q_ref.shape[1]
    fresh = vb_ref.shape[1]
    found = dot(x_ref[...], w_ref[...], NN)
    q_ref[...] = (found[:, :width] + qb_ref[...]).astype(jnp.bfloat16)
    k_ref[...] = found[:, width : 2 * width].astype(jnp.bfloat16)
    values = (found[:, 2 * width :] + vb_ref[...]).astype(jnp.bfloat16)
    reused = reused_ref[...]
    for head in range(fresh // HD):
        part = slice(head * HD, (head + 1) * HD)
        v_ref[:, 2 * head * HD : 2 * (head + 1) * HD] = jnp.concatenate(
            [values[:, part], reused[:, part]], axis=1
        )


def project(normed, weight, query_bias, value_bias, reused):
    rows, depth = normed.shape
    width, fresh = query_bias.shape[0], value_bias.shape[0]
    out = pl.BlockSpec((BLOCK, width), lambda i: (i, 0))
    return pl.pallas_call(
        project_kernel,
        grid=(rows // BLOCK,),
        in_specs=[
            pl.BlockSpec((BLOCK, depth), lambda i: (i, 0)),
            pl.BlockSpec(weight.shape, lambda i: (0, 0)),
            pl.BlockSpec((1, width), lambda i: (0, 0)),
            pl.BlockSpec((1, fresh), lambda i: (0, 0)),
            pl.BlockSpec((BLOCK, fresh), lambda i: (i, 0)),
        ],
        out_specs=[out] * 3,
        out_shape=[jax.ShapeDtypeStruct((rows, width), jnp.bfloat16)] * 3,
        compiler_params=pltpu.CompilerParams(vmem_limit_bytes=VMEM_BYTES),
        cost_estimate=HINT,
    )(normed, weight, query_bias[None], value_bias[None], reused)


def fresh_columns(values):
    return jnp.concatenate(
        [values[:, k * HD : (k + 1) * HD] for k in range(0, values.shape[1] // HD, 2)], axis=1
    )


def reused_columns(values):
    return jnp.concatenate(
        [values[:, k * HD : (k + 1) * HD] for k in range(1, values.shape[1] // HD, 2)], axis=1
    )


def last_weights_kernel(x_ref, dq_ref, dk_ref, dv_ref, wo_ref, out_ref, q_sum_ref, v_sum_ref):
    size, half = dq_ref.shape[1], wo_ref.shape[1] // 2
    out_ref[:size, :half] = wo_ref[:, :half]
    out_ref[size:, :half] = wo_ref[:, half:]
    x = x_ref[...]
    out_ref[:, half : half + size] = dot(x, dq_ref[...], TN).astype(jnp.bfloat16)
    out_ref[:, half + size : half + 2 * size] = dot(x, dk_ref[...], TN).astype(jnp.bfloat16)
    fresh = fresh_columns(dv_ref[...])
    out_ref[:, half + 2 * size :] = dot(x, fresh, TN).astype(jnp.bfloat16)
    q_sum_ref[...] = jnp.sum(dq_ref[...].astype(jnp.float32), axis=0, keepdims=True)
    v_sum_ref[...] = jnp.sum(fresh.astype(jnp.float32), axis=0, keepdims=True)


def last_weights(normed, query_grad, key_grad, value_grad, w_out_grad):
    width, size = normed.shape[1], query_grad.shape[1]
    return pl.pallas_call(
        last_weights_kernel,
        out_shape=[
            jax.ShapeDtypeStruct((width, width // 2 + 5 * size // 2), jnp.bfloat16),
            jax.ShapeDtypeStruct((1, size), jnp.float32),
            jax.ShapeDtypeStruct((1, size // 2), jnp.float32),
        ],
        compiler_params=pltpu.CompilerParams(vmem_limit_bytes=VMEM_BYTES),
        cost_estimate=HINT,
    )(normed, query_grad, key_grad, value_grad, w_out_grad)


def inputs_back_kernel(side_ref, *refs):
    w_ref, keep_ref, send_ref, keep_reused_ref, send_reused_ref = refs[6:]
    for (dq_ref, dk_ref, dv_ref), out_ref, reused_ref in (
        (refs[0:3], keep_ref, keep_reused_ref),
        (refs[3:6], send_ref, send_reused_ref),
    ):
        size = dq_ref.shape[1]
        total = dot(dq_ref[...], w_ref[:, :size], NT) + dot(
            dk_ref[...], w_ref[:, size : 2 * size], NT
        )
        total = total + dot(fresh_columns(dv_ref[...]), w_ref[:, 2 * size :], NT)
        out_ref[...] = total.astype(out_ref.dtype)
        reused_ref[...] = reused_columns(dv_ref[...])


def inputs_back(side, query_grad, key_grad, value_grad, w_in):
    rows, size = query_grad.shape
    half, width = rows // 2, w_in.shape[0]
    blocks = half // BLOCK
    keep = pl.BlockSpec((BLOCK, size), lambda i, side: (side[0] * blocks + i, 0))
    send = pl.BlockSpec((BLOCK, size), lambda i, side: ((1 - side[0]) * blocks + i, 0))
    out = pl.BlockSpec((BLOCK, width), lambda i, side: (i, 0))
    out_reused = pl.BlockSpec((BLOCK, size // 2), lambda i, side: (i, 0))
    return pl.pallas_call(
        inputs_back_kernel,
        grid_spec=pltpu.PrefetchScalarGridSpec(
            num_scalar_prefetch=1,
            grid=(blocks,),
            in_specs=[keep] * 3 + [send] * 3 + [pl.BlockSpec(w_in.shape, lambda i, side: (0, 0))],
            out_specs=[out, out, out_reused, out_reused],
        ),
        out_shape=[
            jax.ShapeDtypeStruct((half, width), jnp.float32),
            jax.ShapeDtypeStruct((half, width), jnp.bfloat16),
            jax.ShapeDtypeStruct((half, size // 2), jnp.bfloat16),
            jax.ShapeDtypeStruct((half, size // 2), jnp.bfloat16),
        ],
        compiler_params=pltpu.CompilerParams(vmem_limit_bytes=VMEM_BYTES),
        cost_estimate=HINT,
    )(
        jnp.reshape(side, (1,)),
        query_grad,
        key_grad,
        value_grad,
        query_grad,
        key_grad,
        value_grad,
        w_in,
    )


def product(left, right):
    return dot(left, right, NN)


def shards(
    tokens,
    first_values,
    lengths,
    reuse_index,
    ln1_gain,
    ln1_bias,
    w_query,
    query_bias,
    w_key,
    w_value,
    value_bias,
    w_out,
    out_bias,
    ln2_gain,
    ln2_bias,
    w_up,
    up_bias,
    w_down,
    down_bias,
    cotangent,
):
    place, side = lax.axis_index("dp"), lax.axis_index("tensor")
    core = place % 2
    local_rows, width = tokens.shape
    rows = 2 * local_rows
    query_size, value_size = query_bias.shape[0], value_bias.shape[0]
    fresh_here = value_size // HD
    length = lengths[0]
    positions = side * local_rows + jnp.arange(local_rows)
    valid_rows = (positions < length).astype(jnp.float32)[:, None]

    inputs = tokens.astype(jnp.float32)
    normed_one = norm_rows(inputs, ln1_gain, ln1_bias).astype(jnp.bfloat16)
    got_one = across(normed_one)
    early, late = cotangent[: local_rows // 2], cotangent[local_rows // 2 :]
    got_early = across(early)
    picks = reuse_index[jnp.arange(2 * value_size) // HD]
    selector = (
        (jnp.arange(width)[:, None] // HD == picks[None, :])
        & ((jnp.arange(width) % HD)[:, None] == (jnp.arange(2 * value_size) % HD)[None, :])
    ).astype(jnp.bfloat16)
    first_values, selector = after((first_values, selector), normed_one)
    chosen = product(first_values, selector).astype(jnp.bfloat16)
    own_chosen, other_chosen = slabs(chosen, side)
    got_chosen = across(other_chosen)
    gathered_one = join(normed_one, got_one, side)
    reused = join(own_chosen, got_chosen, side)
    w_in = jnp.concatenate([w_query, w_key, w_value], axis=1)

    out_grad = cotangent.astype(jnp.float32) * valid_rows
    down_bias_grad = jnp.sum(out_grad, axis=0)
    branch_grad = out_grad.astype(jnp.bfloat16)
    out_piece, late = after((halves(w_out, core)[0], late), got_one, got_chosen)
    got_out = across(out_piece)
    got_late = across(late)
    other_positions = (1 - side) * local_rows + jnp.arange(local_rows)
    got_branch_grad = jnp.where(
        (other_positions < length)[:, None], jnp.concatenate([got_early, got_late], axis=0), 0
    )

    queries, keys, values = project(gathered_one, w_in, query_bias, value_bias, reused)
    heads_out, lse = attend(lengths, queries, keys, values, local_rows)
    w_out_other = join(got_out, flip(got_out, 1), core)
    heads_keep, heads_send = halves(heads_out, side)
    heads_got = across(heads_send)
    attention = product(heads_keep, w_out) + product(heads_got, w_out_other)
    middle = inputs + attention + out_bias
    normed_two = norm_rows(middle, ln2_gain, ln2_bias).astype(jnp.bfloat16)
    got_two = across(normed_two)
    own = feed(normed_two, branch_grad, w_up, up_bias, w_down)
    got_two, own = lax.optimization_barrier((got_two, own))
    other = feed(got_two, got_branch_grad, w_up, up_bias, w_down)
    up_bias_grad = (own[4] + other[4])[0]
    back_got = across(other[1].astype(jnp.bfloat16))
    chains = []
    for part in range(PARTS):
        weights = feed_weights(
            part,
            (own[2], other[2]),
            (own[3], other[3]),
            (normed_two, got_two),
            (branch_grad, got_branch_grad),
        )
        chains.append(Chain(weights.reshape(-1, width), place))
    advance(chains, [1, 0])
    (branch_send,) = after((other[0].astype(jnp.bfloat16),), back_got)
    back_got = hold(chains, back_got)
    normed_two_grad = own[1] + back_got.astype(jnp.float32)
    _, norm_two_back = jax.vjp(norm_rows, middle, ln2_gain, ln2_bias)
    middle_part, ln2_gain_grad, ln2_bias_grad = norm_two_back(normed_two_grad)
    middle_grad = out_grad + middle_part
    out_bias_grad = jnp.sum(middle_grad, axis=0)
    attention_grad = middle_grad.astype(jnp.bfloat16)
    heads_grad_got = across(dot(attention_grad, w_out_other, NT).astype(jnp.bfloat16))
    heads_grad = join(dot(attention_grad, w_out, NT).astype(jnp.bfloat16), heads_grad_got, side)
    out_grad_got = across(dot(heads_got, attention_grad, TN).astype(jnp.bfloat16))
    w_out_part = dot(heads_keep, attention_grad, TN)
    advance(chains, [1, 1])
    heads_grad, branch_send = hold(chains, heads_grad, branch_send)
    query_grad, key_grad, value_grad = attend_back(
        lengths, queries, keys, values, heads_out, lse, heads_grad, local_rows
    )
    w_out_grad = (w_out_part + out_grad_got.astype(jnp.float32)).astype(jnp.bfloat16)
    last, query_sums, value_sums = last_weights(
        gathered_one, query_grad, key_grad, value_grad, w_out_grad
    )
    query_bias_grad, value_bias_grad = query_sums[0], value_sums[0]
    chains.append(Chain(last, place))
    one_keep, one_send, first_keep, first_send = inputs_back(
        side, query_grad, key_grad, value_grad, w_in
    )
    branch_got = across(branch_send)
    advance(chains, [2, 1, 0])
    one_send, first_send, branch_got = hold(chains, one_send, first_send, branch_got)
    one_got = across(one_send)
    first_got = across(first_send)
    advance(chains, [2, 2, 2])
    one_got, first_got = hold(chains, one_got, first_got)
    result = (
        (middle + own[0] + branch_got.astype(jnp.float32) + down_bias) * valid_rows
    ).astype(jnp.bfloat16)
    normed_one_grad = one_keep + one_got.astype(jnp.float32)
    first_grads = jnp.concatenate(
        [jnp.where(side == 0, first_keep, first_got), jnp.where(side == 0, first_got, first_keep)],
        axis=1,
    )
    first_values_grad = dot(first_grads, selector, NT)
    _, norm_one_back = jax.vjp(norm_rows, inputs, ln1_gain, ln1_bias)
    input_part, ln1_gain_grad, ln1_bias_grad = norm_one_back(normed_one_grad)
    tokens_grad = middle_grad + input_part
    whole = jnp.concatenate(
        [ln1_gain_grad, ln1_bias_grad, out_bias_grad, ln2_gain_grad, ln2_bias_grad, down_bias_grad]
    )
    whole = whole + across(whole)
    small = jnp.concatenate([whole, query_bias_grad, value_bias_grad, up_bias_grad])
    bits = dp_bits()
    for bit in bits[:1]:
        small = small + flip(small, bit)
    advance(chains, [1, 2, 2])
    small, result, tokens_grad, first_values_grad = hold(
        chains, small, result, tokens_grad, first_values_grad
    )
    for bit in bits[1:3]:
        small = small + flip(small, bit)
    advance(chains, [1, 1, 2])
    small = hold(chains, small)
    for bit in bits[3:]:
        small = small + flip(small, bit)
    advance(chains, [0, 1, 1])
    feeds = [chain.finish().astype(jnp.float32) for chain in chains[:PARTS]]
    w_down_grad = jnp.concatenate([f[: f.shape[0] // 2] for f in feeds], axis=0)
    w_up_grad = jnp.concatenate([f[f.shape[0] // 2 :] for f in feeds], axis=1)
    chains[PARTS].values, w_down_grad, w_up_grad, small = lax.optimization_barrier(
        (chains[PARTS].values, w_down_grad, w_up_grad, small)
    )
    ln1_gain_grad, ln1_bias_grad, out_bias_grad, ln2_gain_grad, ln2_bias_grad, down_bias_grad = (
        small[k * width : (k + 1) * width] for k in range(6)
    )
    query_bias_grad = small[6 * width : 6 * width + query_size]
    value_bias_grad = small[6 * width + query_size : 6 * width + query_size + value_size]
    up_bias_grad = small[6 * width + query_size + value_size :]
    half = width // 2
    last = chains[PARTS].finish().astype(jnp.float32)
    w_out_grad = jnp.concatenate([last[:query_size, :half], last[query_size:, :half]], axis=1)
    w_query_grad = last[:, half : half + query_size]
    w_key_grad = last[:, half + query_size : half + 2 * query_size]
    w_value_grad = last[:, half + 2 * query_size :]
    return (
        result,
        tokens_grad,
        first_values_grad,
        ln1_gain_grad,
        ln1_bias_grad,
        w_query_grad,
        query_bias_grad,
        w_key_grad,
        w_value_grad,
        value_bias_grad,
        w_out_grad,
        out_bias_grad,
        ln2_gain_grad,
        ln2_bias_grad,
        w_up_grad,
        up_bias_grad,
        w_down_grad,
        down_bias_grad,
    )


def solution(mesh):
    in_specs = (
        P(("dp", "tensor"), None),
        P(("dp", "tensor"), None),
        P("dp"),
        P(),
        P(),
        P(),
        P(None, "tensor"),
        P("tensor"),
        P(None, "tensor"),
        P(None, "tensor"),
        P("tensor"),
        P("tensor", None),
        P(),
        P(),
        P(),
        P(None, "tensor"),
        P("tensor"),
        P("tensor", None),
        P(),
        P(("dp", "tensor"), None),
    )
    out_specs = (
        P(("dp", "tensor"), None),
        P(("dp", "tensor"), None),
        P(("dp", "tensor"), None),
        P(),
        P(),
        P(None, "tensor"),
        P("tensor"),
        P(None, "tensor"),
        P(None, "tensor"),
        P("tensor"),
        P("tensor", None),
        P(),
        P(),
        P(),
        P(None, "tensor"),
        P("tensor"),
        P("tensor", None),
        P(),
    )
    return jax.shard_map(shards, mesh=mesh, in_specs=in_specs, out_specs=out_specs, check_vma=False)
```

time: 724 us -> 351 us (0.48)
  waiting for transfers between devices: 378 us -> 139 us
  matrix products: 117 us -> 6.53 us
  blocking collectives: 102 us -> 0 us
  Pallas kernels: 0 us -> 69.6 us
  starting transfers between devices: 0.8 us -> 39.2 us
  between operations: 15.5 us -> 2.92 us
  loops' own time: 8.43 us -> 0 us
    psum x1 -> x0, waiting for transfers between devices: 178 us -> none  [shards(): lax.psum((w_query_grad, query_bias_grad, w_key_grad, w_value_grad, value_...]
    ppermute x0 -> x43, waiting for transfers between devices: none -> 139 us  [the longest x14 72.1 us: across(): return lax.ppermute(values, 'tensor', [(0, 1), (1, 0)])]
    all_gather x5 -> x0, waiting for transfers between devices: 128 us -> none  [the longest x1 27.5 us: shards(): lax.all_gather(normed_one, 'tensor', axis=0, tiled=True)]
    dot_general x34 -> x8, matrix products: 117 us -> 6.53 us  [dot(): lax.dot_general(left, right, dims, preferred_element_type=jnp.float32)]
    psum x2 -> x0, blocking collectives: 102 us -> none  [the longest x1 62.7 us: shards(): lax.psum((w_query_grad, query_bias_grad, w_key_grad, w_value_grad, value_...]
    reduce_scatter x5 -> x0, waiting for transfers between devices: 71.1 us -> none  [the longest x1 25.8 us: shards(): lax.psum_scatter(product(heads_out, w_out).astype(jnp.bfloat16), 'tensor'...]
    pallas_call x0 -> x9, Pallas kernels: none -> 69.6 us  [the longest x2 22.3 us: feed(): pl.pallas_call(feed_kernel, grid=(hidden // tile,), in_specs=[whole, whol...]
    ppermute x0 -> x43, starting transfers between devices: none -> 39.2 us  [the longest x29 25.7 us: flip(): lax.ppermute(values, 'dp', [(d, d ^ bit) for d in range(lax.axis_size('dp...]
  transfers between devices with their start and end apart: 11 -> 43, of which waited for: 9 -> 22; matrix products, arithmetic and copies ran while one was open for 8% -> 13% of each run, Pallas kernels for 0% -> 15%
where the time goes in v1:
time: 351 us; the launch traced here: 347 us
  waiting for transfers between devices  139 us (40%)
  Pallas kernels  69.6 us (20%)
  other arithmetic  56.6 us (16%)
  starting transfers between devices  39.2 us (11%)
  local copies, waits for them, and re-layouts  32.5 us (9%)
  matrix products  6.53 us (2%)
    ppermute x14, waiting for transfers between devices, across(): return lax.ppermute(values, 'tensor', [(0, 1), (1, 0)])  72.1 us
    ppermute x29, waiting for transfers between devices, flip(): lax.ppermute(values, 'dp', [(d, d ^ bit) for d in range(lax.axis_size('dp...  67.2 us
    ppermute x29, starting transfers between devices, flip(): lax.ppermute(values, 'dp', [(d, d ^ bit) for d in range(lax.axis_size('dp...  25.7 us
    pallas_call x2, Pallas kernels, feed(): pl.pallas_call(feed_kernel, grid=(hidden // tile,), in_specs=[whole, whol...  22.3 us
    pallas_call x1, Pallas kernels, attend_back(): pl.pallas_call(partial(attend_back_kernel, sure), grid_spec=pltpu.Prefetc...  13.7 us
    ppermute x14, starting transfers between devices, across(): return lax.ppermute(values, 'tensor', [(0, 1), (1, 0)])  13.4 us
    pallas_call x2, Pallas kernels, feed_weights(): pl.pallas_call(partial(feed_weights_kernel, hidden // BLOCK), grid=(1,),...  13 us
    pallas_call x1, Pallas kernels, attend(): pl.pallas_call(partial(attend_kernel, sure), grid_spec=pltpu.PrefetchScal...  9.92 us
  transfers between devices with their start and end apart: 43, of which 22 were waited for; matrix products, arithmetic and copies ran while one was open for 13% of the time, Pallas kernels for 15%

profile of v1, /device:TPU:0, one launch (start us, length us, event | category | flops | bytes accessed | tf_op | source)
XLA Modules:
  0.0 346.6 jit_solution(323405787515428111)
XLA Ops:
  4.9 3.0 collective-permute-start
  8.5 3.9 %fusion.39 = s32[384]{0:T(512)S(1)} fusion(s32[]{:T(128)} %bitcast.1, s32[]{:T(128)} %bitcast.2, s32[]{:T(128)} %bitcast.3, s32[]{:T(128)} %bitcast.4, s32[]{:T(128)} %bitcast.6, s32[]{:T(128)} %bitcast.5), kind=kLoop, calls=%fused_computation.176 | loop fusion | flops 8064 | bytes 1560 | tf_op jit(solution)/shard_map/gather | solution.py:497
  20.0 11.3 %collective-permute-done.1 = bf16[512,192]{1,0:T(8,128)(2,1)} collective-permute-done((bf16[512,192]{1,0:T(8,128)(2,1)}, bf16[512,192]{1,0:T(8,128)(2,1)}, u32[]{:S(2)}, u32[]{:S(2)}) %collective-permute-start.1) | collective-permute-done | bytes 196640 | tf_op jit(solution)/shard_map/ppermute | solution.py:24
  36.9 3.1 shard_map.331
  40.0 9.9 %shard_map.332 = (bf16[1024,384]{1,0:T(8,128)(2,1)S(1)}, f32[3,2,1024]{2,1,0:T(2,128)S(1)}) custom-call(s32[1]{0:T(128)} %copy.59.length_ref, bf16[1024,384]{1,0:T(8,128)(2,1)S(1)} %get-tuple-element.89.q_ref, bf16[1024,384]{1,0:T(8,128)(2,1)S(1)} %get-tuple-element.90.k_ref, bf16[1024,384]{1,0:T(8,128)(2,1)S(1)} %get-tuple-element.91.v_ref), custom_call_target="tpu_custom_call" | custom-call | flops 1048576 | bytes 65536 | tf_op jit(solution)/shard_map/pallas_call | solution.py:161
  51.7 10.0 %collective-permute-done.2 = bf16[512,384]{1,0:T(8,128)(2,1)S(1)} collective-permute-done((bf16[512,384]{1,0:T(8,128)(2,1)S(1)}, bf16[512,384]{1,0:T(8,128)(2,1)S(1)}, u32[]{:S(2)}, u32[]{:S(2)}) %collective-permute-start.2) | collective-permute-done | bytes 393248 | tf_op jit(solution)/shard_map/ppermute | solution.py:24
  68.1 25.4 %collective-permute-done.6 = bf16[256,768]{1,0:T(8,128)(2,1)S(1)} collective-permute-done((bf16[256,768]{1,0:T(8,128)(2,1)}, bf16[256,768]{1,0:T(8,128)(2,1)S(1)}, u32[]{:S(2)}, u32[]{:S(2)}) %collective-permute-start.6) | collective-permute-done | bytes 393248 | tf_op jit(solution)/shard_map/ppermute | solution.py:24
  94.3 6.5 %collective-permute-done.7 = bf16[256,768]{1,0:T(8,128)(2,1)} collective-permute-done((bf16[256,768]{1,0:T(8,128)(2,1)}, bf16[256,768]{1,0:T(8,128)(2,1)}, u32[]{:S(2)}, u32[]{:S(2)}) %collective-permute-start.7) | collective-permute-done | bytes 393248 | tf_op jit(solution)/shard_map/ppermute | solution.py:24
  102.1 11.1 %shard_map.333 = (f32[512,768]{1,0:T(8,128)S(1)}, f32[512,768]{1,0:T(8,128)S(1)}, bf16[512,1536]{1,0:T(8,128)(2,1)}, bf16[512,1536]{1,0:T(8,128)(2,1)}, f32[1,1536]{1,0:T(1,128)S(1)}) custom-call(bf16[512,768]{1,0:T(8,128)(2,1)} %add_convert_fusion.3.normed_ref.refs_4_, bf16[512,768]{1,0:T(8,128)(2,1)S(1)} %fusion.13.grad_ref.refs_6_, ...), custom_call_target="tpu_custom_call" | custom-call | flops 1048576 | bytes 65536 | tf_op jit(solution)/shard_map/pallas_call | solution.py:280
  115.5 11.3 %shard_map.334 = (f32[512,768]{1,0:T(8,128)S(1)}, f32[512,768]{1,0:T(8,128)S(1)}, bf16[512,1536]{1,0:T(8,128)(2,1)}, bf16[512,1536]{1,0:T(8,128)(2,1)}, f32[1,1536]{1,0:T(1,128)S(1)}) custom-call(bf16[512,768]{1,0:T(8,128)(2,1)} %collective-permute-done.5.normed_ref.refs_5_, bf16[512,768]{1,0:T(8,128)(2,1)S(1)} %maximum_select_fusion.grad_ref.refs_7_, ...), custom_call_target="tpu_custom_call" | custom-call | flops 1048576 | bytes 65536 | tf_op jit(solution)/shard_map/pallas_call | solution.py:280
  126.8 6.7 %shard_map.335 = bf16[2,768,768]{2,1,0:T(8,128)(2,1)} custom-call(bf16[512,1536]{1,0:T(8,128)(2,1)S(1)} %copy-done.5, bf16[512,1536]{1,0:T(8,128)(2,1)} %get-tuple-element.102.refs_1_, bf16[512,1536]{1,0:T(8,128)(2,1)} %get-tuple-element.103.refs_2_, bf16[512,1536]{1,0:T(8,128)(2,1)} %get-tuple-element.104.refs_3_, ...), custom_call_target="tpu_custom_call" | custom-call | flops 1048576 | bytes 65536 | tf_op jit(solution)/shard_map/pallas_call | solution.py:319
  139.0 6.3 %shard_map.336 = bf16[2,768,768]{2,1,0:T(8,128)(2,1)} custom-call(bf16[512,1536]{1,0:T(8,128)(2,1)S(1)} %copy-done.6, bf16[512,1536]{1,0:T(8,128)(2,1)} %get-tuple-element.102.refs_1_, bf16[512,1536]{1,0:T(8,128)(2,1)} %get-tuple-element.103.refs_2_, bf16[512,1536]{1,0:T(8,128)(2,1)} %get-tuple-element.104.refs_3_, ...), custom_call_target="tpu_custom_call" | custom-call | flops 1048576 | bytes 65536 | tf_op jit(solution)/shard_map/pallas_call | solution.py:319
  145.3 11.8 %collective-permute-done.9 = bf16[512,768]{1,0:T(8,128)(2,1)} collective-permute-done((bf16[512,768]{1,0:T(8,128)(2,1)}, bf16[512,768]{1,0:T(8,128)(2,1)}, u32[]{:S(2)}, u32[]{:S(2)}) %collective-permute-start.9) | collective-permute-done | bytes 786464 | tf_op jit(solution)/shard_map/ppermute | solution.py:24
  169.7 7.0 %collective-permute-done.12 = bf16[512,384]{1,0:T(8,128)(2,1)S(1)} collective-permute-done((bf16[512,384]{1,0:T(8,128)(2,1)S(1)}, bf16[512,384]{1,0:T(8,128)(2,1)S(1)}, u32[]{:S(2)}, u32[]{:S(2)}) %collective-permute-start.12) | collective-permute-done | bytes 393248 | tf_op jit(solution)/shard_map/ppermute | solution.py:24
  177.8 3.9 %collective-permute-done.10 = bf16[384,768]{1,0:T(8,128)(2,1)S(1)} collective-permute-done((bf16[384,768]{1,0:T(8,128)(2,1)S(1)}, bf16[384,768]{1,0:T(8,128)(2,1)S(1)}, u32[]{:S(2)}, u32[]{:S(2)}) %collective-permute-start.10) | collective-permute-done | bytes 589856 | tf_op jit(solution)/shard_map/ppermute | solution.py:28
  187.1 3.8 %collective-permute-done.13 = bf16[192,768]{1,0:T(8,128)(2,1)S(1)} collective-permute-done((bf16[192,768]{1,0:T(8,128)(2,1)S(1)}, bf16[192,768]{1,0:T(8,128)(2,1)S(1)}, u32[]{:S(2)}, u32[]{:S(2)}) %collective-permute-start.13) | collective-permute-done | bytes 294944 | tf_op jit(solution)/shard_map/ppermute | solution.py:28
  191.0 2.7 collective-permute-start.14
  193.9 13.7 %shard_map.337 = (bf16[1024,384]{1,0:T(8,128)(2,1)S(1)}, bf16[1024,384]{1,0:T(8,128)(2,1)S(1)}, bf16[1024,384]{1,0:T(8,128)(2,1)S(1)}) custom-call(s32[1]{0:T(128)} %copy.59.length_ref, bf16[1024,384]{1,0:T(8,128)(2,1)S(1)} %copy-done.10, bf16[1024,384]{1,0:T(8,128)(2,1)S(1)} %copy-done.12, bf16[1024,384]{1,0:T(8,128)(2,1)S(1)} %copy-done.14, ...), custom_call_target="tpu_custom_call" | custom-call | flops 1048576 | bytes 65536 | tf_op jit(solution)/shard_map/pallas_call | solution.py:220
  207.6 3.9 %shard_map.339 = (f32[512,768]{1,0:T(8,128)S(1)}, bf16[512,768]{1,0:T(8,128)(2,1)S(1)}, bf16[512,192]{1,0:T(8,128)(2,1)S(1)}, bf16[512,192]{1,0:T(8,128)(2,1)S(1)}) custom-call(s32[1]{0:T(128)} %bitcast.10.side_ref, bf16[1024,384]{1,0:T(8,128)(2,1)S(1)} %get-tuple-element.116.dq_ref.refs_0_.refs_3_, ...), custom_call_target="tpu_custom_call" | custom-call | flops 1048576 | bytes 65536 | tf_op jit(solution)/shard_map/pallas_call | solution.py:428
  211.5 3.6 %shard_map.338 = (bf16[768,1344]{1,0:T(8,128)(2,1)}, f32[1,384]{1,0:T(1,128)S(1)}, f32[1,192]{1,0:T(1,128)S(1)}) custom-call(bf16[1024,768]{1,0:T(8,128)(2,1)S(1)} %pad_maximum_fusion.3.x_ref, bf16[1024,384]{1,0:T(8,128)(2,1)S(1)} %get-tuple-element.116.dq_ref.refs_0_.refs_3_, bf16[1024,384]{1,0:T(8,128)(2,1)S(1)} %get-tuple-element.117.dk_ref.refs_1_.refs_4_, ...), custom_call_target="tpu_custom_call" | custom-call | flops 1048576 | bytes 65536 | tf_op jit(solution)/shard_map/pallas_call | solution.py:393
  225.6 5.5 %collective-permute-done.18 = bf16[96,768]{1,0:T(8,128)(2,1)} collective-permute-done((bf16[96,768]{1,0:T(8,128)(2,1)S(1)}, bf16[96,768]{1,0:T(8,128)(2,1)}, u32[]{:S(2)}, u32[]{:S(2)}) %collective-permute-start.18) | collective-permute-done | bytes 147488 | tf_op jit(solution)/shard_map/ppermute | solution.py:28
  247.7 8.0 %collective-permute-done.23 = bf16[192,1344]{1,0:T(8,128)(2,1)S(1)} collective-permute-done((bf16[192,1344]{1,0:T(8,128)(2,1)S(1)}, bf16[192,1344]{1,0:T(8,128)(2,1)S(1)}, u32[]{:S(2)}, u32[]{:S(2)}) %collective-permute-start.23) | collective-permute-done | bytes 516128 | tf_op jit(solution)/shard_map/ppermute | solution.py:28
  271.3 2.8 collective-permute-done.29
  277.7 3.8 %collective-permute-done.30 = bf16[48,1344]{1,0:T(8,128)(2,1)S(1)} collective-permute-done((bf16[48,1344]{1,0:T(8,128)(2,1)S(1)}, bf16[48,1344]{1,0:T(8,128)(2,1)S(1)}, u32[]{:S(2)}, u32[]{:S(2)}) %collective-permute-start.30) | collective-permute-done | bytes 129056 | tf_op jit(solution)/shard_map/ppermute | solution.py:28
  281.5 4.6 %collective-permute-done.28 = bf16[192,768]{1,0:T(8,128)(2,1)S(1)} collective-permute-done((bf16[192,768]{1,0:T(8,128)(2,1)S(1)}, bf16[192,768]{1,0:T(8,128)(2,1)S(1)}, u32[]{:S(2)}, u32[]{:S(2)}) %collective-permute-start.28) | collective-permute-done | bytes 294944 | tf_op jit(solution)/shard_map/ppermute | solution.py:28
  287.6 8.0 %collective-permute-done.35 = bf16[48,1344]{1,0:T(8,128)(2,1)S(1)} collective-permute-done((bf16[48,1344]{1,0:T(8,128)(2,1)S(1)}, bf16[48,1344]{1,0:T(8,128)(2,1)S(1)}, u32[]{:S(2)}, u32[]{:S(2)}) %collective-permute-start.35) | collective-permute-done | bytes 129056 | tf_op jit(solution)/shard_map/ppermute | solution.py:28
  296.7 3.0 collective-permute-done.37
  304.3 10.5 %collective-permute-done.34 = bf16[384,768]{1,0:T(8,128)(2,1)S(1)} collective-permute-done((bf16[384,768]{1,0:T(8,128)(2,1)S(1)}, bf16[384,768]{1,0:T(8,128)(2,1)S(1)}, u32[]{:S(2)}, u32[]{:S(2)}) %collective-permute-start.34) | collective-permute-done | bytes 589856 | tf_op jit(solution)/shard_map/ppermute | solution.py:28
  317.1 4.6 %collective-permute-done.41 = f32[6720]{0:T(1024)S(1)} collective-permute-done((f32[6720]{0:T(1024)S(1)}, f32[6720]{0:T(1024)S(1)}, u32[]{:S(2)}, u32[]{:S(2)}) %collective-permute-start.41) | collective-permute-done | bytes 26912 | tf_op jit(solution)/shard_map/ppermute | solution.py:28
  321.7 4.9 %collective-permute-done.39 = bf16[192,1344]{1,0:T(8,128)(2,1)S(1)} collective-permute-done((bf16[192,1344]{1,0:T(8,128)(2,1)S(1)}, bf16[192,1344]{1,0:T(8,128)(2,1)S(1)}, u32[]{:S(2)}, u32[]{:S(2)}) %collective-permute-start.39) | collective-permute-done | bytes 516128 | tf_op jit(solution)/shard_map/ppermute | solution.py:28
  327.7 2.9 pad_maximum_fusion.1
  341.9 3.3 fusion.48
  (334 shorter events, 122.7 us)
Async XLA Ops:
  4.9 27.7 %collective-permute-start = (bf16[512,768]{1,0:T(8,128)(2,1)}, bf16[512,768]{1,0:T(8,128)(2,1)}, u32[]{:S(2)}, u32[]{:S(2)}) collective-permute-start(bf16[512,768]{1,0:T(8,128)(2,1)} %fusion.7), channel_id=1, source_target_pairs={{0,1},{1,0},{2,3},{3,2},{4,5},{5,4},{6,7},{7,6},{8,9},{9,8},{10,11... | collective-permute-start | bytes 2359304 | tf_op jit(solution)/shard_map/ppermute | solution.py:24
  15.9 15.5 %collective-permute-start.1 = (bf16[512,192]{1,0:T(8,128)(2,1)}, bf16[512,192]{1,0:T(8,128)(2,1)}, u32[]{:S(2)}, u32[]{:S(2)}) collective-permute-start(bf16[512,192]{1,0:T(8,128)(2,1)} %constant_dynamic-slice_fusion.14), channel_id=1, source_target_pairs={{0,1},{1,0},{2,3},{3,2},{4,5},{5,4},{6,7},{7,6},{8,9},{9,8},{10,11... | collective-permute-start | bytes 589832 | tf_op jit(solution)/shard_map/ppermute | solution.py:24
  32.7 17.3 %collective-permute-start.3 = (bf16[192,768]{1,0:T(8,128)(2,1)S(1)}, bf16[192,768]{1,0:T(8,128)(2,1)S(1)}, u32[]{:S(2)}, u32[]{:S(2)}) collective-permute-start(bf16[192,768]{1,0:T(8,128)(2,1)S(1)} %copy-done.56), channel_id=1, source_target_pairs={{0,1},{1,0},{2,3},{3,2},{4,5},{5,4},{6,7},{7,6},{8,9},{9,8},{10,11... | collective-permute-start | bytes 884744 | tf_op jit(solution)/shard_map/ppermute | solution.py:24
  50.2 11.6 %collective-permute-start.2 = (bf16[512,384]{1,0:T(8,128)(2,1)S(1)}, bf16[512,384]{1,0:T(8,128)(2,1)S(1)}, u32[]{:S(2)}, u32[]{:S(2)}) collective-permute-start(bf16[512,384]{1,0:T(8,128)(2,1)S(1)} %constant_dynamic-slice_fusion.13), channel_id=1, source_target_pairs={{0,1},{1,0},{2,3},{3,2},{4,5},{5,4},{6,7},{7,6},{8,9},{9,8},{10,11... | collective-permute-start | bytes 1179656 | tf_op jit(solution)/shard_map/ppermute | solution.py:24
  64.4 51.0 %collective-permute-start.5 = (bf16[512,768]{1,0:T(8,128)(2,1)}, bf16[512,768]{1,0:T(8,128)(2,1)}, u32[]{:S(2)}, u32[]{:S(2)}) collective-permute-start(bf16[512,768]{1,0:T(8,128)(2,1)} %add_convert_fusion.3.normed_ref.refs_4_), channel_id=1, source_target_pairs={{0,1},{1,0},{2,3},{3,2},{4,5},{5,4},{6,7},{7,6},{8,9},{9,8},{10,11... | collective-permute-start | bytes 2359304 | tf_op jit(solution)/shard_map/ppermute | solution.py:24
  64.7 28.8 %collective-permute-start.6 = (bf16[256,768]{1,0:T(8,128)(2,1)}, bf16[256,768]{1,0:T(8,128)(2,1)S(1)}, u32[]{:S(2)}, u32[]{:S(2)}) collective-permute-start(bf16[256,768]{1,0:T(8,128)(2,1)} %get-tuple-element.247), channel_id=1, source_target_pairs={{0,1},{1,0},{2,3},{3,2},{4,5},{5,4},{6,7},{7,6},{8,9},{9,8},{10,11... | collective-permute-start | bytes 1179656 | tf_op jit(solution)/shard_map/ppermute | solution.py:24
  66.5 34.3 %collective-permute-start.7 = (bf16[256,768]{1,0:T(8,128)(2,1)}, bf16[256,768]{1,0:T(8,128)(2,1)}, u32[]{:S(2)}, u32[]{:S(2)}) collective-permute-start(bf16[256,768]{1,0:T(8,128)(2,1)} %get-tuple-element.101), channel_id=1, source_target_pairs={{0,1},{1,0},{2,3},{3,2},{4,5},{5,4},{6,7},{7,6},{8,9},{9,8},{10,11... | collective-permute-start | bytes 1179656 | tf_op jit(solution)/shard_map/ppermute | solution.py:24
  135.8 21.2 %collective-permute-start.8 = (bf16[768,768]{1,0:T(8,128)(2,1)}, bf16[768,768]{1,0:T(8,128)(2,1)}, u32[]{:S(2)}, u32[]{:S(2)}) collective-permute-start(bf16[768,768]{1,0:T(8,128)(2,1)} %constant_dynamic-slice_fusion.11), channel_id=1, source_target_pairs={{0,2},{2,0},{4,6},{6,4},{8,10},{10,8},{12,14},{14,12},{16,18},{18,... | collective-permute-start | bytes 3538952 | tf_op jit(solution)/shard_map/ppermute | solution.py:28
  136.8 20.3 %collective-permute-start.9 = (bf16[512,768]{1,0:T(8,128)(2,1)}, bf16[512,768]{1,0:T(8,128)(2,1)}, u32[]{:S(2)}, u32[]{:S(2)}) collective-permute-start(bf16[512,768]{1,0:T(8,128)(2,1)} %convert_element_type.194), channel_id=1, source_target_pairs={{0,1},{1,0},{2,3},{3,2},{4,5},{5,4},{6,7},{7,6},{8,9},{9,8},{10,11... | collective-permute-start | bytes 2359304 | tf_op jit(solution)/shard_map/ppermute | solution.py:24
  164.6 12.1 %collective-permute-start.12 = (bf16[512,384]{1,0:T(8,128)(2,1)S(1)}, bf16[512,384]{1,0:T(8,128)(2,1)S(1)}, u32[]{:S(2)}, u32[]{:S(2)}) collective-permute-start(bf16[512,384]{1,0:T(8,128)(2,1)S(1)} %convolution_convert_fusion.1), channel_id=1, source_target_pairs={{0,1},{1,0},{2,3},{3,2},{4,5},{5,4},{6,7},{7,6},{8,9},{9,8},{10,11... | collective-permute-start | bytes 1179656 | tf_op jit(solution)/shard_map/ppermute | solution.py:24
  165.8 16.1 %collective-permute-start.11 = (bf16[768,768]{1,0:T(8,128)(2,1)S(1)}, bf16[768,768]{1,0:T(8,128)(2,1)S(1)}, u32[]{:S(2)}, u32[]{:S(2)}) collective-permute-start(bf16[768,768]{1,0:T(8,128)(2,1)S(1)} %constant_dynamic-slice_fusion.9), channel_id=1, source_target_pairs={{0,2},{2,0},{4,6},{6,4},{8,10},{10,8},{12,14},{14,12},{16,18},{18,... | collective-permute-start | bytes 3538952 | tf_op jit(solution)/shard_map/ppermute | solution.py:28
  165.9 15.8 %collective-permute-start.10 = (bf16[384,768]{1,0:T(8,128)(2,1)S(1)}, bf16[384,768]{1,0:T(8,128)(2,1)S(1)}, u32[]{:S(2)}, u32[]{:S(2)}) collective-permute-start(bf16[384,768]{1,0:T(8,128)(2,1)S(1)} %constant_dynamic-slice_fusion.10), channel_id=1, source_target_pairs={{0,4},{2,6},{4,0},{6,2},{8,12},{10,14},{12,8},{14,10},{16,20},{18,... | collective-permute-start | bytes 1769480 | tf_op jit(solution)/shard_map/ppermute | solution.py:28
  168.0 25.7 %collective-permute-start.16 = (bf16[384,768]{1,0:T(8,128)(2,1)S(1)}, bf16[384,768]{1,0:T(8,128)(2,1)S(1)}, u32[]{:S(2)}, u32[]{:S(2)}) collective-permute-start(bf16[384,768]{1,0:T(8,128)(2,1)S(1)} %convolution_convert_fusion), channel_id=1, source_target_pairs={{0,1},{1,0},{2,3},{3,2},{4,5},{5,4},{6,7},{7,6},{8,9},{9,8},{10,11... | collective-permute-start | bytes 1769480 | tf_op jit(solution)/shard_map/ppermute | solution.py:24
  182.2 8.7 %collective-permute-start.13 = (bf16[192,768]{1,0:T(8,128)(2,1)S(1)}, bf16[192,768]{1,0:T(8,128)(2,1)S(1)}, u32[]{:S(2)}, u32[]{:S(2)}) collective-permute-start(bf16[192,768]{1,0:T(8,128)(2,1)S(1)} %constant_dynamic-slice_fusion.8), channel_id=1, source_target_pairs={{0,8},{2,10},{4,12},{6,14},{8,0},{10,2},{12,4},{14,6},{16,24},{18,... | collective-permute-start | bytes 884744 | tf_op jit(solution)/shard_map/ppermute | solution.py:28
  184.5 30.7 %collective-permute-start.15 = (bf16[384,768]{1,0:T(8,128)(2,1)S(1)}, bf16[384,768]{1,0:T(8,128)(2,1)S(1)}, u32[]{:S(2)}, u32[]{:S(2)}) collective-permute-start(bf16[384,768]{1,0:T(8,128)(2,1)S(1)} %constant_dynamic-slice_fusion.6), channel_id=1, source_target_pairs={{0,4},{2,6},{4,0},{6,2},{8,12},{10,14},{12,8},{14,10},{16,20},{18,... | collective-permute-start | bytes 1769480 | tf_op jit(solution)/shard_map/ppermute | solution.py:28
  186.0 30.1 %collective-permute-start.17 = (bf16[512,768]{1,0:T(8,128)(2,1)S(1)}, bf16[512,768]{1,0:T(8,128)(2,1)S(1)}, u32[]{:S(2)}, u32[]{:S(2)}) collective-permute-start(bf16[512,768]{1,0:T(8,128)(2,1)S(1)} %convert_element_type.205), channel_id=1, source_target_pairs={{0,1},{1,0},{2,3},{3,2},{4,5},{5,4},{6,7},{7,6},{8,9},{9,8},{10,11... | collective-permute-start | bytes 2359304 | tf_op jit(solution)/shard_map/ppermute | solution.py:24
  191.0 24.1 %collective-permute-start.14 = (bf16[96,768]{1,0:T(8,128)(2,1)S(1)}, bf16[96,768]{1,0:T(8,128)(2,1)S(1)}, u32[]{:S(2)}, u32[]{:S(2)}) collective-permute-start(bf16[96,768]{1,0:T(8,128)(2,1)S(1)} %constant_dynamic-slice_fusion.7), channel_id=1, source_target_pairs={{0,16},{2,18},{4,20},{6,22},{8,24},{10,26},{12,28},{14,30},{16,0},... | collective-permute-start | bytes 442376 | tf_op jit(solution)/shard_map/ppermute | solution.py:28
  220.5 17.6 %collective-permute-start.22 = (bf16[384,1344]{0,1:T(8,128)(2,1)}, bf16[384,1344]{0,1:T(8,128)(2,1)}, u32[]{:S(2)}, u32[]{:S(2)}) collective-permute-start(bf16[384,1344]{0,1:T(8,128)(2,1)} %copy.46), channel_id=1, source_target_pairs={{0,2},{2,0},{4,6},{6,4},{8,10},{10,8},{12,14},{14,12},{16,18},{18,... | collective-permute-start | bytes 3096584 | tf_op jit(solution)/shard_map/ppermute | solution.py:28
  220.5 10.5 %collective-permute-start.18 = (bf16[96,768]{1,0:T(8,128)(2,1)S(1)}, bf16[96,768]{1,0:T(8,128)(2,1)}, u32[]{:S(2)}, u32[]{:S(2)}) collective-permute-start(bf16[96,768]{1,0:T(8,128)(2,1)S(1)} %add_convert_fusion.12), channel_id=1, source_target_pairs={{0,16},{2,18},{4,20},{6,22},{8,24},{10,26},{12,28},{14,30},{16,0},... | collective-permute-start | bytes 442376 | tf_op jit(solution)/shard_map/ppermute | solution.py:28
  221.9 12.1 %collective-permute-start.20 = (bf16[192,768]{1,0:T(8,128)(2,1)S(1)}, bf16[192,768]{1,0:T(8,128)(2,1)S(1)}, u32[]{:S(2)}, u32[]{:S(2)}) collective-permute-start(bf16[192,768]{1,0:T(8,128)(2,1)S(1)} %constant_dynamic-slice_fusion.5), channel_id=1, source_target_pairs={{0,8},{2,10},{4,12},{6,14},{8,0},{10,2},{12,4},{14,6},{16,24},{18,... | collective-permute-start | bytes 884744 | tf_op jit(solution)/shard_map/ppermute | solution.py:28
  223.5 32.4 %collective-permute-start.24 = (bf16[512,768]{1,0:T(8,128)(2,1)S(1)}, bf16[512,768]{1,0:T(8,128)(2,1)}, u32[]{:S(2)}, u32[]{:S(2)}) collective-permute-start(bf16[512,768]{1,0:T(8,128)(2,1)S(1)} %copy-done.20), channel_id=1, source_target_pairs={{0,1},{1,0},{2,3},{3,2},{4,5},{5,4},{6,7},{7,6},{8,9},{9,8},{10,11... | collective-permute-start | bytes 2359304 | tf_op jit(solution)/shard_map/ppermute | solution.py:24
  224.6 31.3 %collective-permute-start.25 = (bf16[512,192]{1,0:T(8,128)(2,1)S(1)}, bf16[512,192]{1,0:T(8,128)(2,1)}, u32[]{:S(2)}, u32[]{:S(2)}) collective-permute-start(bf16[512,192]{1,0:T(8,128)(2,1)S(1)} %copy-done.22), channel_id=1, source_target_pairs={{0,1},{1,0},{2,3},{3,2},{4,5},{5,4},{6,7},{7,6},{8,9},{9,8},{10,11... | collective-permute-start | bytes 589832 | tf_op jit(solution)/shard_map/ppermute | solution.py:24
  232.7 11.4 %collective-permute-start.19 = (bf16[192,768]{1,0:T(8,128)(2,1)}, bf16[192,768]{1,0:T(8,128)(2,1)}, u32[]{:S(2)}, u32[]{:S(2)}) collective-permute-start(bf16[192,768]{1,0:T(8,128)(2,1)} %pad_maximum_fusion.17), channel_id=1, source_target_pairs={{0,8},{2,10},{4,12},{6,14},{8,0},{10,2},{12,4},{14,6},{16,24},{18,... | collective-permute-start | bytes 884744 | tf_op jit(solution)/shard_map/ppermute | solution.py:28
  235.8 10.3 %collective-permute-start.21 = (bf16[96,768]{1,0:T(8,128)(2,1)S(1)}, bf16[96,768]{1,0:T(8,128)(2,1)}, u32[]{:S(2)}, u32[]{:S(2)}) collective-permute-start(bf16[96,768]{1,0:T(8,128)(2,1)S(1)} %constant_dynamic-slice_fusion.4), channel_id=1, source_target_pairs={{0,16},{2,18},{4,20},{6,22},{8,24},{10,26},{12,28},{14,30},{16,0},... | collective-permute-start | bytes 442376 | tf_op jit(solution)/shard_map/ppermute | solution.py:28
  242.6 13.1 %collective-permute-start.23 = (bf16[192,1344]{1,0:T(8,128)(2,1)S(1)}, bf16[192,1344]{1,0:T(8,128)(2,1)S(1)}, u32[]{:S(2)}, u32[]{:S(2)}) collective-permute-start(bf16[192,1344]{1,0:T(8,128)(2,1)S(1)} %constant_dynamic-slice_fusion.2), channel_id=1, source_target_pairs={{0,4},{2,6},{4,0},{6,2},{8,12},{10,14},{12,8},{14,10},{16,20},{18,... | collective-permute-start | bytes 1548296 | tf_op jit(solution)/shard_map/ppermute | solution.py:28
  263.9 10.2 %collective-permute-start.29 = (bf16[96,1344]{1,0:T(8,128)(2,1)S(1)}, bf16[96,1344]{1,0:T(8,128)(2,1)S(1)}, u32[]{:S(2)}, u32[]{:S(2)}) collective-permute-start(bf16[96,1344]{1,0:T(8,128)(2,1)S(1)} %constant_dynamic-slice_fusion.1), channel_id=1, source_target_pairs={{0,8},{2,10},{4,12},{6,14},{8,0},{10,2},{12,4},{14,6},{16,24},{18,... | collective-permute-start | bytes 774152 | tf_op jit(solution)/shard_map/ppermute | solution.py:28
  266.9 19.4 %collective-permute-start.26 = (bf16[384,768]{1,0:T(8,128)(2,1)}, bf16[384,768]{1,0:T(8,128)(2,1)S(1)}, u32[]{:S(2)}, u32[]{:S(2)}) collective-permute-start(bf16[384,768]{1,0:T(8,128)(2,1)} %pad_maximum_fusion.11), channel_id=1, source_target_pairs={{0,4},{2,6},{4,0},{6,2},{8,12},{10,14},{12,8},{14,10},{16,20},{18,... | collective-permute-start | bytes 1769480 | tf_op jit(solution)/shard_map/ppermute | solution.py:28
  275.5 10.7 %collective-permute-start.28 = (bf16[192,768]{1,0:T(8,128)(2,1)S(1)}, bf16[192,768]{1,0:T(8,128)(2,1)S(1)}, u32[]{:S(2)}, u32[]{:S(2)}) collective-permute-start(bf16[192,768]{1,0:T(8,128)(2,1)S(1)} %pad_maximum_fusion.18), channel_id=1, source_target_pairs={{0,8},{2,10},{4,12},{6,14},{8,0},{10,2},{12,4},{14,6},{16,24},{18,... | collective-permute-start | bytes 884744 | tf_op jit(solution)/shard_map/ppermute | solution.py:28
  296.7 18.3 %collective-permute-start.33 = (bf16[768,768]{1,0:T(8,128)(2,1)S(1)}, bf16[768,768]{1,0:T(8,128)(2,1)S(1)}, u32[]{:S(2)}, u32[]{:S(2)}) collective-permute-start(bf16[768,768]{1,0:T(8,128)(2,1)S(1)} %pad_maximum_fusion.5), channel_id=1, source_target_pairs={{0,2},{2,0},{4,6},{6,4},{8,10},{10,8},{12,14},{14,12},{16,18},{18,... | collective-permute-start | bytes 3538952 | tf_op jit(solution)/shard_map/ppermute | solution.py:28
  301.6 13.2 %collective-permute-start.34 = (bf16[384,768]{1,0:T(8,128)(2,1)S(1)}, bf16[384,768]{1,0:T(8,128)(2,1)S(1)}, u32[]{:S(2)}, u32[]{:S(2)}) collective-permute-start(bf16[384,768]{1,0:T(8,128)(2,1)S(1)} %pad_maximum_fusion.12), channel_id=1, source_target_pairs={{0,4},{2,6},{4,0},{6,2},{8,12},{10,14},{12,8},{14,10},{16,20},{18,... | collective-permute-start | bytes 1769480 | tf_op jit(solution)/shard_map/ppermute | solution.py:28
  315.3 11.3 %collective-permute-start.39 = (bf16[192,1344]{1,0:T(8,128)(2,1)S(1)}, bf16[192,1344]{1,0:T(8,128)(2,1)S(1)}, u32[]{:S(2)}, u32[]{:S(2)}) collective-permute-start(bf16[192,1344]{1,0:T(8,128)(2,1)S(1)} %pad_maximum_fusion.13), channel_id=1, source_target_pairs={{0,4},{2,6},{4,0},{6,2},{8,12},{10,14},{12,8},{14,10},{16,20},{18,... | collective-permute-start | bytes 1548296 | tf_op jit(solution)/shard_map/ppermute | solution.py:28
  316.7 10.1 %collective-permute-start.40 = (bf16[768,768]{1,0:T(8,128)(2,1)S(1)}, bf16[768,768]{1,0:T(8,128)(2,1)S(1)}, u32[]{:S(2)}, u32[]{:S(2)}) collective-permute-start(bf16[768,768]{1,0:T(8,128)(2,1)S(1)} %pad_maximum_fusion.6), channel_id=1, source_target_pairs={{0,2},{2,0},{4,6},{6,4},{8,10},{10,8},{12,14},{14,12},{16,18},{18,... | collective-permute-start | bytes 3538952 | tf_op jit(solution)/shard_map/ppermute | solution.py:28
  (79 other events, 453.0 us)

commit v2 on v1

v2 whole, which is shorter than its diff:
```python
from functools import partial

import jax
import jax.numpy as jnp
from jax import lax
from jax.experimental import pallas as pl
from jax.experimental.pallas import tpu as pltpu
from jax.sharding import PartitionSpec as P

H = 12
HD = 64
PARTS = 2
BLOCK = 256
VMEM_BYTES = 24 * 1024 * 1024
NT = (((1,), (1,)), ((), ()))
TN = (((0,), (0,)), ((), ()))
NN = (((1,), (0,)), ((), ()))
F32 = jnp.float32
BF16 = jnp.bfloat16
STRETCH = 15
SIDE, LENGTH, CORE, WHICH = 0, 1, 2, 3


def shape(dims, dtype):
    return jax.ShapeDtypeStruct(dims, dtype)


def call(kernel, scalars, arrays, out_shape, in_specs=None, out_specs=None, grid=(1,), scratch=(), micros=2):
    def whole(array):
        return pl.BlockSpec(array.shape, lambda *_, dims=len(array.shape): (0,) * dims)

    return pl.pallas_call(
        kernel,
        grid_spec=pltpu.PrefetchScalarGridSpec(
            num_scalar_prefetch=1,
            grid=grid,
            in_specs=[s or whole(a) for s, a in zip(in_specs or [None] * len(arrays), arrays)],
            out_specs=[
                s or whole(o) for s, o in zip(out_specs or [None] * len(out_shape), out_shape)
            ],
            scratch_shapes=list(scratch),
        ),
        out_shape=out_shape,
        compiler_params=pltpu.CompilerParams(vmem_limit_bytes=VMEM_BYTES),
        cost_estimate=pl.CostEstimate(
            flops=STRETCH * micros * 1_150_000_000,
            bytes_accessed=STRETCH * micros * 3_600_000,
            transcendentals=0,
        ),
    )(scalars, *arrays)


def dot(left, right, dims=NN):
    return lax.dot_general(left, right, dims, preferred_element_type=F32)


def pick(flag, left, right):
    return jnp.where(flag, left.astype(F32), right.astype(F32)).astype(left.dtype)


def across(values):
    return lax.ppermute(values, "tensor", [(0, 1), (1, 0)])


def flip(values, bit):
    return lax.ppermute(values, "dp", [(d, d ^ bit) for d in range(lax.axis_size("dp"))])


def halves(values, which):
    half = values.shape[0] // 2
    return (
        lax.dynamic_slice_in_dim(values, which * half, half, 0),
        lax.dynamic_slice_in_dim(values, (1 - which) * half, half, 0),
    )


def join(own, other, which):
    return jnp.concatenate(
        [jnp.where(which == 0, own, other), jnp.where(which == 0, other, own)], axis=0
    )


def slabs(values, which):
    half = values.shape[1] // 2
    return (
        lax.dynamic_slice_in_dim(values, which * half, half, 1),
        lax.dynamic_slice_in_dim(values, (1 - which) * half, half, 1),
    )


def after(values, *found):
    return lax.optimization_barrier((values, found))[0]


def dp_bits():
    return [1 << k for k in range(lax.axis_size("dp").bit_length() - 1)]


def parts_of(refs):
    if len(refs) > 1:
        return list(refs)
    return [refs[0].at[p] for p in range(refs[0].shape[0])]


def fold_kernel(n_got, scalars, own_ref, *refs):
    gots, keep_ref, sends = parts_of(refs[:n_got]), refs[n_got], parts_of(refs[n_got + 1 :])
    half = keep_ref.shape[1]
    which = scalars[0]
    for p, (got_ref, send_ref) in enumerate(zip(gots, sends)):
        for out_ref, part in ((keep_ref.at[p], which), (send_ref, 1 - which)):
            rows = pl.ds(pl.multiple_of(part * half, half), half)
            total = own_ref[p, rows, :].astype(F32) + got_ref[rows, :].astype(F32)
            out_ref[...] = total.astype(BF16)


def join_kernel(n_own, n_got, scalars, *refs):
    owns, gots = parts_of(refs[:n_own]), parts_of(refs[n_own : n_own + n_got])
    outs = parts_of(refs[n_own + n_got :])
    which = scalars[0]
    for own_ref, got_ref, out_ref in zip(owns, gots, outs):
        half = own_ref.shape[0]
        for in_ref, part in ((own_ref, which), (got_ref, 1 - which)):
            out_ref[pl.ds(pl.multiple_of(part * half, half), half), :] = in_ref[...]


class Chain:
    def __init__(self, keep, send, parts, place, split):
        self.keep, self.sends, self.gots = keep, (send,), ()
        self.parts, self.place, self.split = parts, place, split
        bits = dp_bits()
        self.steps = []
        for bit, following in zip(bits, bits[1:] + [0]):
            self.steps += [("halve", bit, following)] * (parts if split and bit == 2 else 1)
        for bit in reversed(bits):
            self.steps += [("double", bit, bit // 2)] * (parts if split and bit == 2 else 1)

    @property
    def state(self):
        return (self.keep, self.sends, self.gots)

    @state.setter
    def state(self, values):
        self.keep, self.sends, self.gots = values

    def which(self, bit):
        return (self.place // bit) % 2

    def shapes(self, rows, columns, bit):
        if self.split and bit == 2:
            return [shape((rows, columns), BF16)] * self.parts
        return [shape((self.parts, rows, columns), BF16)]

    def step(self):
        if not self.steps:
            return
        kind, bit, following = self.steps.pop(0)
        self.gots += (flip(self.sends[len(self.gots)], bit),)
        if len(self.gots) < len(self.sends):
            return
        gots, self.gots = self.gots, ()
        rows, columns = gots[0].shape[-2:]
        if kind == "halve" and not following:
            total = self.keep.astype(F32) + gots[0].astype(F32)
            self.keep, self.sends = None, (total.astype(BF16),)
        elif kind == "halve" and (rows // 2) % 16:
            total = (self.keep.astype(F32) + gots[0].astype(F32)).astype(BF16)
            self.keep, send = (
                lax.dynamic_slice_in_dim(total, w * (rows // 2), rows // 2, 1)
                for w in (self.which(following), 1 - self.which(following))
            )
            self.sends = (send,)
        elif kind == "halve":
            whole = [pl.BlockSpec(g.shape, lambda *_, d=g.ndim: (0,) * d) for g in gots]
            kept = pl.BlockSpec((self.parts, rows, columns), lambda *_: (0, 0, 0))
            self.keep, *sends = call(
                partial(fold_kernel, len(gots)),
                self.which(following)[None],
                [self.keep, *gots],
                [shape((self.parts, rows // 2, columns), BF16)]
                + self.shapes(rows // 2, columns, following),
                [kept, *whole],
            )
            self.sends = tuple(sends)
        elif not following:
            self.gots = gots
        elif rows % 16:
            own, got, w = self.sends[0], gots[0], self.which(bit)
            self.sends = (
                jnp.concatenate(
                    [jnp.where(w == 0, own, got), jnp.where(w == 0, got, own)], axis=1
                ),
            )
        else:
            self.sends = tuple(
                call(
                    partial(join_kernel, len(self.sends), len(gots)),
                    self.which(bit)[None],
                    [*self.sends, *gots],
                    self.shapes(2 * rows, columns, following),
                )
            )


def advance(chains, counts):
    for chain, count in zip(chains, counts):
        for _ in range(count):
            chain.step()


def hold(chains, *values):
    states, values = lax.optimization_barrier(([c.state for c in chains], values))
    for chain, state in zip(chains, states):
        chain.state = state
    return values if len(values) != 1 else values[0]


def unit_rows(values):
    centred = values - jnp.mean(values, axis=-1, keepdims=True)
    spread = jnp.mean(centred * centred, axis=-1, keepdims=True)
    scale = lax.rsqrt(spread + 1e-05)
    return centred * scale, scale


def unit_rows_back(unit, scale, grad):
    inner = jnp.mean(grad * unit, axis=-1, keepdims=True)
    return scale * (grad - jnp.mean(grad, axis=-1, keepdims=True) - unit * inner)


def column_sum(values):
    return jnp.sum(values, axis=0, keepdims=True)


def row_spec(width, place=lambda i: i):
    return pl.BlockSpec((BLOCK, width), lambda i, scalars: (place(i), 0))


def valid_rows(scalars, block, rows):
    position = scalars[SIDE] * rows + block * BLOCK
    position = position + lax.broadcasted_iota(jnp.int32, (BLOCK, 1), 0)
    return (position < scalars[LENGTH]).astype(F32)


def norm_kernel(scalars, x_ref, gain_ref, bias_ref, out_ref):
    unit, _ = unit_rows(x_ref[...].astype(F32))
    out_ref[...] = (unit * gain_ref[...] + bias_ref[...]).astype(BF16)


def norm(scalars, values, gain, bias):
    rows, width = values.shape
    return call(
        norm_kernel,
        scalars,
        [values, gain[None], bias[None]],
        [shape((rows, width), BF16)],
        [row_spec(width), None, None],
        [row_spec(width)],
        (rows // BLOCK,),
    )[0]


def project_kernel(
    scalars, x_ref, x_got_ref, w_ref, qb_ref, vb_ref, reused_ref, reused_got_ref, q_ref, k_ref, v_ref
):
    width, fresh = q_ref.shape[1], vb_ref.shape[1]
    own = pl.program_id(0) < pl.num_programs(0) // 2

    def work(x_ref, reused_ref):
        found = dot(x_ref[...], w_ref[...])
        q_ref[...] = (found[:, :width] + qb_ref[...]).astype(BF16)
        k_ref[...] = found[:, width : 2 * width].astype(BF16)
        values = (found[:, 2 * width :] + vb_ref[...]).astype(BF16)
        reused = reused_ref[...]
        for head in range(fresh // HD):
            part = slice(head * HD, (head + 1) * HD)
            v_ref[:, 2 * head * HD : 2 * (head + 1) * HD] = jnp.concatenate(
                [values[:, part], reused[:, part]], axis=1
            )

    pl.when(own)(lambda: work(x_ref, reused_ref))
    pl.when(jnp.logical_not(own))(lambda: work(x_got_ref, reused_got_ref))


def project(scalars, normed, normed_got, weight, query_bias, value_bias, reused, reused_got):
    local, depth = normed.shape
    width, fresh = query_bias.shape[0], value_bias.shape[0]
    blocks = local // BLOCK
    x_spec, r_spec = (row_spec(w, lambda i: jnp.minimum(i, blocks - 1)) for w in (depth, fresh))
    x_got_spec, r_got_spec = (
        row_spec(w, lambda i: jnp.maximum(i - blocks, 0)) for w in (depth, fresh)
    )
    out_spec = pl.BlockSpec(
        (BLOCK, width),
        lambda i, scalars: (lax.rem(i + scalars[SIDE] * blocks, 2 * blocks), 0),
    )
    return call(
        project_kernel,
        scalars,
        [normed, normed_got, weight, query_bias[None], value_bias[None], reused, reused_got],
        [shape((2 * local, width), BF16)] * 3,
        [x_spec, x_got_spec, None, None, None, r_spec, r_got_spec],
        [out_spec] * 3,
        (2 * blocks,),
        micros=4,
    )


def mix_kernel(
    scalars, keep_ref, got_ref, w_ref, w_other_ref, x_ref, ob_ref, gain_ref, bias_ref, mid_ref, out_ref
):
    attention = dot(keep_ref[...], w_ref[...]) + dot(got_ref[...], w_other_ref[...])
    middle = x_ref[...].astype(F32) + attention + ob_ref[...]
    mid_ref[...] = middle
    unit, _ = unit_rows(middle)
    out_ref[...] = (unit * gain_ref[...] + bias_ref[...]).astype(BF16)


def mix(scalars, keep, got, w_out, w_out_other, tokens, out_bias, gain, bias):
    rows, width = tokens.shape
    half, whole = row_spec(got.shape[1]), row_spec(width)
    kept = pl.BlockSpec((None, BLOCK, got.shape[1]), lambda i, scalars: (0, i, 0))
    return call(
        mix_kernel,
        scalars,
        [keep, got, w_out, w_out_other, tokens, out_bias[None], gain[None], bias[None]],
        [shape((rows, width), F32), shape((rows, width), BF16)],
        [kept, half, None, None, whole, None, None, None],
        [whole, whole],
        (rows // BLOCK,),
        micros=3,
    )


def turn_kernel(
    scalars,
    mid_ref,
    cot_ref,
    back_ref,
    back_got_ref,
    gain_ref,
    w_ref,
    w_other_ref,
    mid_grad_ref,
    grad_ref,
    own_ref,
    send_ref,
    sums_ref,
):
    block = pl.program_id(0)
    rows = pl.num_programs(0) * BLOCK
    out_grad = cot_ref[...].astype(F32) * valid_rows(scalars, block, rows)
    unit, scale = unit_rows(mid_ref[...])
    normed_grad = back_ref[...] + back_got_ref[...].astype(F32)
    middle_grad = out_grad + unit_rows_back(unit, scale, normed_grad * gain_ref[...])
    mid_grad_ref[...] = middle_grad
    grad = middle_grad.astype(BF16)
    grad_ref[...] = grad
    own_ref[...] = dot(grad, w_ref[...], NT).astype(BF16)
    send_ref[...] = dot(grad, w_other_ref[...], NT).astype(BF16)

    @pl.when(block == 0)
    def _():
        sums_ref[...] = jnp.zeros_like(sums_ref)

    for k, part in enumerate((normed_grad * unit, normed_grad, middle_grad, out_grad)):
        sums_ref[k : k + 1, :] += column_sum(part)


def turn(scalars, middle, cotangent, back, back_got, gain, w_out, w_out_other):
    rows, width = middle.shape
    whole, half = row_spec(width), row_spec(w_out.shape[0])
    return call(
        turn_kernel,
        scalars,
        [middle, cotangent, back, back_got, gain[None], w_out, w_out_other],
        [shape((rows, width), F32), shape((rows, width), BF16)]
        + [shape((rows, w_out.shape[0]), BF16)] * 2
        + [shape((8, width), F32)],
        [whole, whole, whole, whole, None, None, None],
        [whole, whole, half, half, None],
        (rows // BLOCK,),
        micros=4,
    )


def close_kernel(
    scalars,
    x_ref,
    gain_ref,
    keep_ref,
    got_ref,
    got_late_ref,
    mid_grad_ref,
    grad_ref,
    sums_ref,
):
    unit, scale = unit_rows(x_ref[...].astype(F32))
    early = pl.program_id(0) < pl.num_programs(0) // 2
    normed_grad = keep_ref[...] + pick(early, got_ref[...], got_late_ref[...]).astype(F32)
    grad_ref[...] = mid_grad_ref[...] + unit_rows_back(unit, scale, normed_grad * gain_ref[...])

    @pl.when(pl.program_id(0) == 0)
    def _():
        sums_ref[...] = jnp.zeros_like(sums_ref)

    for k, part in enumerate((normed_grad * unit, normed_grad)):
        sums_ref[k : k + 1, :] += column_sum(part)


def close(scalars, tokens, gain, keep, got, got_late, middle_grad):
    rows, width = tokens.shape
    whole = row_spec(width)
    last = rows // BLOCK // 2 - 1
    first_half = row_spec(width, lambda i: jnp.minimum(i, last))
    second_half = row_spec(width, lambda i: jnp.maximum(i - last - 1, 0))
    return call(
        close_kernel,
        scalars,
        [tokens, gain[None], keep, got, got_late, middle_grad],
        [shape((rows, width), F32), shape((8, width), F32)],
        [whole, None, whole, first_half, second_half, whole],
        [whole, None],
        (rows // BLOCK,),
        micros=3,
    )


def score_parts(k_ref, query, begin, length, sure):
    parts = []
    for first, last in ((0, begin), (begin, begin + BLOCK)):
        if last > first:
            part = dot(k_ref[first:last, :], query, NT)
            keys = lax.broadcasted_iota(jnp.int32, part.shape, 0) + first
            if first == begin:
                queries = lax.broadcasted_iota(jnp.int32, part.shape, 1) + begin
                part = jnp.where((keys <= queries) & (keys < length), part, -1e30)
            elif last > sure:
                part = jnp.where(keys < length, part, -1e30)
            parts.append((first, last, part))
    return parts


def attend_kernel(scalars, q_ref, k_ref, v_ref, out_ref, lse_ref):
    rows = q_ref.shape[0]
    local = rows // 2
    for begin in range(0, rows, BLOCK):
        query = q_ref[begin : begin + BLOCK, :] * HD ** (-0.5)
        lane = lax.broadcasted_iota(jnp.int32, query.shape, 1)
        mixed = []
        for head in range(2):
            mine = (lane < HD) if head == 0 else (lane >= HD)
            own_query = jnp.where(mine, query, 0).astype(BF16)
            parts = score_parts(k_ref, own_query, begin, scalars[LENGTH], local)
            highest = None
            for _, _, part in parts:
                top = jnp.max(part, axis=0, keepdims=True)
                highest = top if highest is None else jnp.maximum(highest, top)
            total, mixture = 0.0, 0.0
            for first, last, part in parts:
                weights = jnp.exp(part - highest)
                total = total + column_sum(weights)
                mixture = mixture + dot(v_ref[first:last, :], weights.astype(BF16), TN)
            mixed.append(mixture * (1.0 / total))
            lse_ref[0, head : head + 1, begin : begin + BLOCK] = highest + jnp.log(total)
        row = lax.broadcasted_iota(jnp.int32, mixed[0].shape, 0)
        both = jnp.where(row < HD, mixed[0], mixed[1]).T.astype(BF16)
        away = jnp.abs(scalars[SIDE] - begin // local)
        out_ref[away, begin % local : begin % local + BLOCK, :] = both


def pair_spec(rows):
    return pl.BlockSpec((rows, 2 * HD), lambda p, scalars: (0, p))


def sides_spec(rows):
    return pl.BlockSpec((2, rows // 2, 2 * HD), lambda p, scalars: (0, 0, p))


def attend(scalars, queries, keys, values):
    rows, width = queries.shape
    pairs = width // (2 * HD)
    return call(
        attend_kernel,
        scalars,
        [queries, keys, values],
        [shape((2, rows // 2, width), BF16), shape((pairs, 2, rows), F32)],
        [pair_spec(rows)] * 3,
        [sides_spec(rows), pl.BlockSpec((1, 2, rows), lambda p, scalars: (p, 0, 0))],
        (pairs,),
        micros=10,
    )


def attend_back_kernel(
    scalars,
    q_ref,
    k_ref,
    v_ref,
    out_ref,
    lse_ref,
    grad_ref,
    grad_got_ref,
    dq_ref,
    dk_ref,
    dv_ref,
    dk_sum,
    dv_sum,
):
    rows = q_ref.shape[0]
    local = rows // 2
    dk_sum[...] = jnp.zeros_like(dk_sum)
    dv_sum[...] = jnp.zeros_like(dv_sum)
    for begin in range(0, rows, BLOCK):
        block = slice(begin, begin + BLOCK)
        place = slice(begin % local, begin % local + BLOCK)
        here = scalars[SIDE] == begin // local
        query = q_ref[block, :] * HD ** (-0.5)
        grad = pick(here, grad_ref[place, :], grad_got_ref[place, :])
        mixed = out_ref[jnp.abs(scalars[SIDE] - begin // local), place, :]
        product = (grad.astype(F32) * mixed.astype(F32)).T
        lane = lax.broadcasted_iota(jnp.int32, query.shape, 1)
        found = []
        for head in range(2):
            mine = (lane < HD) if head == 0 else (lane >= HD)
            own_query = jnp.where(mine, query, 0).astype(BF16)
            own_grad = jnp.where(mine, grad, 0).astype(BF16)
            inner = column_sum(product[head * HD : (head + 1) * HD, :])
            lse = lse_ref[0, head : head + 1, block]
            query_grad = 0.0
            for first, last, part in score_parts(k_ref, own_query, begin, scalars[LENGTH], local):
                chances = jnp.exp(part - lse)
                chance_grad = dot(v_ref[first:last, :], own_grad, NT)
                score_grad = (chances * (chance_grad - inner)).astype(BF16)
                dv_sum[first:last, :] += dot(chances.astype(BF16), own_grad)
                dk_sum[first:last, :] += dot(score_grad, own_query)
                query_grad = query_grad + dot(k_ref[first:last, :], score_grad, TN)
            found.append(query_grad)
        row = lax.broadcasted_iota(jnp.int32, found[0].shape, 0)
        both = jnp.where(row < HD, found[0], found[1]) * HD ** (-0.5)
        dq_ref[block, :] = both.T.astype(BF16)
    dk_ref[...] = dk_sum[...].astype(BF16)
    dv_ref[...] = dv_sum[...].astype(BF16)


def attend_back(scalars, queries, keys, values, heads_out, lse, grad, grad_got):
    rows, width = queries.shape
    pairs = width // (2 * HD)
    half = pair_spec(rows // 2)
    return call(
        attend_back_kernel,
        scalars,
        [queries, keys, values, heads_out, lse, grad, grad_got],
        [shape((rows, width), BF16)] * 3,
        [pair_spec(rows)] * 3
        + [sides_spec(rows), pl.BlockSpec((1, 2, rows), lambda p, scalars: (p, 0, 0)), half, half],
        [pair_spec(rows)] * 3,
        (pairs,),
        [pltpu.VMEM((rows, 2 * HD), F32)] * 2,
        micros=14,
    )


def gelu_parts(hidden):
    rate = 0.7978845608028654
    square = hidden * hidden
    bend = jnp.tanh(rate * hidden * (1.0 + 0.044715 * square))
    lift = 0.5 * (1.0 + bend)
    slope = lift + 0.5 * hidden * (1.0 - bend * bend) * (rate * (1.0 + 3 * 0.044715 * square))
    return hidden * lift, slope


def feed_kernel(
    scalars,
    normed_ref,
    grad_ref,
    up_ref,
    bias_ref,
    down_ref,
    branch_ref,
    back_ref,
    active_ref,
    hidden_grad_ref,
    bias_grad_ref,
    branch_sum,
    back_sum,
):
    normed, grad = normed_ref[...], grad_ref[...]
    up, down = up_ref[...], down_ref[...]
    active, slope = gelu_parts(dot(normed, up) + bias_ref[...])
    active = active.astype(BF16)
    hidden_grad = (dot(grad, down, NT) * slope).astype(BF16)
    branch, back = dot(active, down), dot(hidden_grad, up, NT)
    active_ref[...] = active
    hidden_grad_ref[...] = hidden_grad
    bias_grad_ref[...] = column_sum(hidden_grad.astype(F32))
    step, last = pl.program_id(0), pl.num_programs(0) - 1

    @pl.when(step == 0)
    def _():
        branch_sum[...] = branch
        back_sum[...] = back

    @pl.when((step > 0) & (step < last))
    def _():
        branch_sum[...] += branch
        back_sum[...] += back

    @pl.when(step == last)
    def _():
        branch_ref[...] = (branch_sum[...] + branch).astype(branch_ref.dtype)
        back_ref[...] = (back_sum[...] + back).astype(back_ref.dtype)


def feed(scalars, normed, grad, w_up, up_bias, w_down, dtype):
    rows, width = normed.shape
    hidden = w_down.shape[0]
    tile = 2 * BLOCK
    part = pl.BlockSpec((rows, tile), lambda i, scalars: (0, i))
    line = pl.BlockSpec((1, tile), lambda i, scalars: (0, i))
    return call(
        feed_kernel,
        scalars,
        [normed, grad, w_up, up_bias[None], w_down],
        [shape((rows, width), dtype)] * 2
        + [shape((rows, hidden), BF16)] * 2
        + [shape((1, hidden), F32)],
        [
            None,
            None,
            pl.BlockSpec((width, tile), lambda i, scalars: (0, i)),
            line,
            pl.BlockSpec((tile, width), lambda i, scalars: (i, 0)),
        ],
        [None, None, part, part, line],
        (hidden // tile,),
        [pltpu.VMEM((rows, width), F32)] * 2,
        micros=10,
    )


def feed_weights_kernel(scalars, *refs):
    actives, hidden_grads, normeds, grads = refs[0:2], refs[2:4], refs[4:6], refs[6:8]
    step = pl.program_id(0)
    per_part = pl.num_programs(0) // PARTS
    down = sum(dot(a[...], g[...], TN) for a, g in zip(actives, grads)).astype(BF16)
    up = sum(dot(n[...], h[...], TN) for n, h in zip(normeds, hidden_grads)).astype(BF16)
    for k in range(PARTS * per_part):
        keep_ref, send_ref = refs[8 + k // per_part * 2 : 10 + k // per_part * 2]
        lines = slice(k % per_part * BLOCK, (k % per_part + 1) * BLOCK)

        @pl.when((step == k) & (scalars[CORE] == 0))
        def _():
            keep_ref[0, lines, :] = down
            send_ref[0, :, lines] = up

        @pl.when((step == k) & (scalars[CORE] == 1))
        def _():
            send_ref[0, lines, :] = down
            keep_ref[0, :, lines] = up


def feed_weights(scalars, actives, hidden_grads, normeds, grads):
    rows, width = normeds[0].shape
    hidden = actives[0].shape[1]
    part = pl.BlockSpec((rows, BLOCK), lambda i, scalars: (0, i))
    return call(
        feed_weights_kernel,
        scalars,
        [*actives, *hidden_grads, *normeds, *grads],
        [shape((1, hidden // PARTS, width), BF16)] * (2 * PARTS),
        [part] * 4 + [None] * 4,
        None,
        (hidden // BLOCK,),
        micros=10,
    )


def fresh_columns(values):
    return jnp.concatenate(
        [values[:, k * HD : (k + 1) * HD] for k in range(0, values.shape[1] // HD, 2)], axis=1
    )


def reused_columns(values):
    return jnp.concatenate(
        [values[:, k * HD : (k + 1) * HD] for k in range(1, values.shape[1] // HD, 2)], axis=1
    )


def last_weights_kernel(
    scalars, x_ref, x_got_ref, dq_ref, dk_ref, dv_ref, wo_ref, wo_got_ref, keep_ref, send_ref, q_sum_ref, v_sum_ref
):
    size, half = dq_ref.shape[1], wo_ref.shape[1] // 2
    local = x_ref.shape[0]
    sides = (scalars[SIDE], 1 - scalars[SIDE])
    spans = [pl.ds(pl.multiple_of(s * local, local), local) for s in sides]
    xs = (x_ref, x_got_ref)
    fresh = [fresh_columns(dv_ref[s, :]) for s in spans]
    for out_ref, h in ((keep_ref, scalars[CORE]), (send_ref, 1 - scalars[CORE])):
        lines = pl.ds(pl.multiple_of(h * half, half), half)
        wo = wo_ref[:, lines] + wo_got_ref[:, lines].astype(F32)
        out_ref[0, :, :half] = wo.astype(BF16)
        for k, d_ref in enumerate((dq_ref, dk_ref)):
            total = sum(dot(x[:, lines], d_ref[s, :], TN) for x, s in zip(xs, spans))
            out_ref[0, :, half + k * size : half + (k + 1) * size] = total.astype(BF16)
        total = sum(dot(x[:, lines], f, TN) for x, f in zip(xs, fresh)).astype(BF16)
        padding = out_ref.shape[2] - half - 2 * size - total.shape[1]
        out_ref[0, :, half + 2 * size :] = jnp.pad(total, ((0, 0), (0, padding)))
    q_sum_ref[...] = column_sum(dq_ref[...].astype(F32))
    v_sum_ref[...] = sum(column_sum(f.astype(F32)) for f in fresh)


def last_weights(scalars, normed, normed_got, query_grad, key_grad, value_grad, wo, wo_got):
    width, size = normed.shape[1], query_grad.shape[1]
    columns = -(-(width // 2 + 5 * size // 2) // 128) * 128
    return call(
        last_weights_kernel,
        scalars,
        [normed, normed_got, query_grad, key_grad, value_grad, wo, wo_got],
        [shape((1, width // 2, columns), BF16)] * 2
        + [shape((1, size), F32), shape((1, size // 2), F32)],
        micros=4,
    )


def inputs_back_kernel(scalars, *refs):
    w_ref, keep_ref, send_ref, keep_reused_ref, send_reused_ref = refs[6:]
    for (dq_ref, dk_ref, dv_ref), out_ref, reused_ref in (
        (refs[0:3], keep_ref, keep_reused_ref),
        (refs[3:6], send_ref, send_reused_ref),
    ):
        size = dq_ref.shape[1]
        total = dot(dq_ref[...], w_ref[:, :size], NT)
        total = total + dot(dk_ref[...], w_ref[:, size : 2 * size], NT)
        total = total + dot(fresh_columns(dv_ref[...]), w_ref[:, 2 * size :], NT)
        out_ref[...] = total.astype(out_ref.dtype)
        reused_ref[...] = reused_columns(dv_ref[...])


def inputs_back(scalars, query_grad, key_grad, value_grad, w_in):
    rows, size = query_grad.shape
    half, width = rows // 2, w_in.shape[0]
    blocks = half // BLOCK
    keep = pl.BlockSpec((BLOCK, size), lambda i, scalars: (scalars[SIDE] * blocks + i, 0))
    send = pl.BlockSpec((BLOCK, size), lambda i, scalars: ((1 - scalars[SIDE]) * blocks + i, 0))
    grads = [query_grad, key_grad, value_grad]
    return call(
        inputs_back_kernel,
        scalars,
        [*grads, *grads, w_in],
        [shape((half, width), F32), shape((half, width), BF16)]
        + [shape((half, size // 2), BF16)] * 2,
        [keep] * 3 + [send] * 3 + [None],
        [row_spec(width)] * 2 + [row_spec(size // 2)] * 2,
        (blocks,),
        micros=4,
    )


def feed_out_kernel(scalars, *refs):
    down_ref, up_ref = refs[-2:]
    first = scalars[CORE] == 0
    for part in range(PARTS):
        own_ref, got_ref = refs[2 * part : 2 * part + 2]

        @pl.when(pl.program_id(0) == part)
        def _():
            own, got = own_ref[0].astype(F32), got_ref[0].astype(F32)
            down_ref[...] = jnp.where(first, own, got)
            up_ref[...] = jnp.where(first, got, own)


def feed_out(scalars, chains):
    arrays = [a for chain in chains for a in (chain.sends[0], chain.gots[0])]
    _, rows, width = arrays[0].shape
    return call(
        feed_out_kernel,
        scalars,
        arrays,
        [shape((PARTS * rows, width), F32), shape((width, PARTS * rows), F32)],
        None,
        [
            pl.BlockSpec((rows, width), lambda i, scalars: (i, 0)),
            pl.BlockSpec((width, rows), lambda i, scalars: (0, i)),
        ],
        (PARTS,),
        micros=5,
    )


def last_out_kernel(scalars, own_ref, got_ref, wo_ref, wq_ref, wk_ref, wv_ref):
    half = own_ref.shape[0]
    size = wq_ref.shape[1]
    first = scalars[CORE] == 0
    own, got = own_ref[...].astype(F32), got_ref[...].astype(F32)
    for h, part in enumerate((jnp.where(first, own, got), jnp.where(first, got, own))):
        lines = slice(h * half, (h + 1) * half)
        wo_ref[:, lines] = part[:, :half]
        wq_ref[lines, :] = part[:, half : half + size]
        wk_ref[lines, :] = part[:, half + size : half + 2 * size]
        wv_ref[:, lines] = part[:, half + 2 * size : half + 2 * size + size // 2].T


def last_out(scalars, chain, size):
    own, got = chain.sends[0][0], chain.gots[0][0]
    half = own.shape[0]
    return call(
        last_out_kernel,
        scalars,
        [own, got],
        [shape((size, 2 * half), F32)]
        + [shape((2 * half, size), F32)] * 2
        + [shape((size // 2, 2 * half), F32)],
        micros=3,
    )


def shards(
    tokens,
    first_values,
    lengths,
    reuse_index,
    ln1_gain,
    ln1_bias,
    w_query,
    query_bias,
    w_key,
    w_value,
    value_bias,
    w_out,
    out_bias,
    ln2_gain,
    ln2_bias,
    w_up,
    up_bias,
    w_down,
    down_bias,
    cotangent,
):
    place, side = lax.axis_index("dp"), lax.axis_index("tensor")
    core = place % 2
    local_rows, width = tokens.shape
    query_size, value_size = query_bias.shape[0], value_bias.shape[0]
    length = lengths[0]
    scalars = jnp.stack([side, length, core]).astype(jnp.int32)
    positions = jnp.arange(local_rows)[:, None]
    own_valid = side * local_rows + positions < length
    other_valid = (1 - side) * local_rows + positions < length

    early, late = cotangent[: local_rows // 2], cotangent[local_rows // 2 :]
    normed_one = norm(scalars, tokens, ln1_gain, ln1_bias)
    one_got = across(normed_one)
    picks = reuse_index[jnp.arange(2 * value_size) // HD]
    selector = (
        (jnp.arange(width)[:, None] // HD == picks[None, :])
        & ((jnp.arange(width) % HD)[:, None] == (jnp.arange(2 * value_size) % HD)[None, :])
    ).astype(BF16)
    first_values, selector = after((first_values, selector), normed_one)
    chosen = dot(first_values, selector).astype(BF16)
    own_chosen, other_chosen = slabs(chosen, side)
    chosen_got = across(other_chosen)
    w_in = jnp.concatenate([w_query, w_key, w_value], axis=1)
    branch_grad = jnp.where(own_valid, cotangent, 0)
    out_piece = halves(w_out, core)[0]
    one_got, chosen_got, w_in, branch_grad, out_piece, early, late = lax.optimization_barrier(
        (one_got, chosen_got, w_in, branch_grad, out_piece, early, late)
    )
    out_got = across(out_piece)
    early_got = across(early)
    queries, keys, values = project(
        scalars, normed_one, one_got, w_in, query_bias, value_bias, own_chosen, chosen_got
    )
    heads_out, lse = attend(scalars, queries, keys, values)
    heads_out, out_got, early_got = lax.optimization_barrier((heads_out, out_got, early_got))
    heads_got = across(heads_out[1])
    w_out_other = join(out_got, flip(out_got, 1), core)
    heads_got, w_out_other, late = lax.optimization_barrier((heads_got, w_out_other, late))
    middle, normed_two = mix(
        scalars, heads_out, heads_got, w_out, w_out_other, tokens, out_bias, ln2_gain, ln2_bias
    )

    normed_two, late = lax.optimization_barrier((normed_two, late))
    two_got = across(normed_two)
    late_got = across(late)
    own = feed(scalars, normed_two, branch_grad, w_up, up_bias, w_down, F32)
    two_got, late_got, own = lax.optimization_barrier((two_got, late_got, own))
    branch_grad_got = jnp.where(other_valid, jnp.concatenate([early_got, late_got], axis=0), 0)
    other = feed(scalars, two_got, branch_grad_got, w_up, up_bias, w_down, BF16)
    up_bias_grad = (own[4] + other[4])[0]
    back_got = across(other[1])
    parts = feed_weights(
        scalars,
        (own[2], other[2]),
        (own[3], other[3]),
        (normed_two, two_got),
        (branch_grad, branch_grad_got),
    )
    chains = [Chain(*parts[2 * k : 2 * k + 2], 1, place, False) for k in range(PARTS)]
    branch_send = other[0]
    back_got, branch_send = hold(chains, back_got, branch_send)

    advance(chains, [1, 1])
    turned = turn(
        scalars, middle, cotangent, own[1], back_got, ln2_gain, w_out, w_out_other
    )
    middle_grad, attention_grad, heads_grad, heads_grad_send, two_sums = hold(chains, *turned)
    heads_grad_got = across(heads_grad_send)
    out_grad_send = dot(heads_got, attention_grad, TN).astype(BF16)
    out_grad_own = dot(heads_out[0], attention_grad, TN)
    advance(chains, [1, 0])
    heads_grad_got, out_grad_send, out_grad_own = hold(
        chains, heads_grad_got, out_grad_send, out_grad_own
    )
    out_grad_got = across(out_grad_send)
    query_grad, key_grad, value_grad = attend_back(
        scalars, queries, keys, values, heads_out, lse, heads_grad, heads_grad_got
    )
    advance(chains, [1, 1])
    middle_rows = local_rows // 2
    out_grad_got, query_grad, key_grad, value_grad, branch_send = hold(
        chains, out_grad_got, query_grad, key_grad, value_grad, branch_send
    )
    keep, send, query_sums, value_sums = last_weights(
        scalars, normed_one, one_got, query_grad, key_grad, value_grad, out_grad_own, out_grad_got
    )
    chains.append(Chain(keep, send, 1, place, False))

    branch_got = across(branch_send[:middle_rows])
    back_keep, back_send, first_keep, first_send = inputs_back(
        scalars, *after((query_grad, key_grad, value_grad), keep), w_in
    )
    advance(chains, [1, 1, 1])
    back_keep, back_send, first_keep, first_send, branch_send, branch_got = hold(
        chains, back_keep, back_send, first_keep, first_send, branch_send, branch_got
    )
    back_got = across(back_send[:middle_rows])
    advance(chains, [1, 1, 1])
    back_got, back_send, first_send = hold(chains, back_got, back_send, first_send)
    back_late = across(back_send[middle_rows:])
    first_got = across(first_send)
    advance(chains, [1, 1, 1])
    back_late, first_got, branch_send = hold(chains, back_late, first_got, branch_send)
    branch_late = across(branch_send[middle_rows:])
    tokens_grad, one_sums = close(
        scalars, tokens, ln1_gain, back_keep, back_got, back_late, middle_grad
    )
    advance(chains, [1, 1, 1])
    tokens_grad, one_sums, branch_late, first_got = hold(
        chains, tokens_grad, one_sums, branch_late, first_got
    )
    first_grads = jnp.concatenate(
        [jnp.where(side == 0, first_keep, first_got), jnp.where(side == 0, first_got, first_keep)],
        axis=1,
    )
    first_values_grad = dot(first_grads, selector, NT)
    whole = jnp.concatenate([one_sums[:2], two_sums[2:3], two_sums[:2], two_sums[3:4]]).reshape(-1)
    whole = whole + across(whole)
    small = jnp.concatenate([whole, query_sums[0], value_sums[0], up_bias_grad])
    bits = dp_bits()
    small = small + flip(small, 1)
    advance(chains, [1, 1, 1])
    small, first_values_grad = hold(chains, small, first_values_grad)
    small = small + flip(small, bits[1])
    small = small + flip(small, bits[2])
    advance(chains, [0, 1, 1])
    small = hold(chains, small)
    for bit in bits[3:]:
        small = small + flip(small, bit)
    branch_all = jnp.concatenate([branch_got, branch_late], axis=0).astype(F32)
    result = (middle + own[0] + branch_all + down_bias) * own_valid.astype(F32)
    result = result.astype(BF16)
    advance(chains, [99, 99, len(chains[2].steps) - 1])
    w_down_grad, w_up_grad = feed_out(scalars, chains[:PARTS])
    chains[-1].state, w_down_grad, w_up_grad, small, result = lax.optimization_barrier(
        (chains[-1].state, w_down_grad, w_up_grad, small, result)
    )
    advance(chains, [0, 0, 1])
    w_out_grad, w_query_grad, w_key_grad, w_value_grad = last_out(scalars, chains[-1], query_size)
    w_value_grad = w_value_grad.T
    ln1_gain_grad, ln1_bias_grad, out_bias_grad, ln2_gain_grad, ln2_bias_grad, down_bias_grad = (
        small[k * width : (k + 1) * width] for k in range(6)
    )
    query_bias_grad = small[6 * width : 6 * width + query_size]
    value_bias_grad = small[6 * width + query_size : 6 * width + query_size + value_size]
    up_bias_grad = small[6 * width + query_size + value_size :]
    return (
        result,
        tokens_grad,
        first_values_grad,
        ln1_gain_grad,
        ln1_bias_grad,
        w_query_grad,
        query_bias_grad,
        w_key_grad,
        w_value_grad,
        value_bias_grad,
        w_out_grad,
        out_bias_grad,
        ln2_gain_grad,
        ln2_bias_grad,
        w_up_grad,
        up_bias_grad,
        w_down_grad,
        down_bias_grad,
    )


def solution(mesh):
    in_specs = (
        P(("dp", "tensor"), None),
        P(("dp", "tensor"), None),
        P("dp"),
        P(),
        P(),
        P(),
        P(None, "tensor"),
        P("tensor"),
        P(None, "tensor"),
        P(None, "tensor"),
        P("tensor"),
        P("tensor", None),
        P(),
        P(),
        P(),
        P(None, "tensor"),
        P("tensor"),
        P("tensor", None),
        P(),
        P(("dp", "tensor"), None),
    )
    out_specs = (
        P(("dp", "tensor"), None),
        P(("dp", "tensor"), None),
        P(("dp", "tensor"), None),
        P(),
        P(),
        P(None, "tensor"),
        P("tensor"),
        P(None, "tensor"),
        P(None, "tensor"),
        P("tensor"),
        P("tensor", None),
        P(),
        P(),
        P(),
        P(None, "tensor"),
        P("tensor"),
        P("tensor", None),
        P(),
    )
    return jax.shard_map(shards, mesh=mesh, in_specs=in_specs, out_specs=out_specs, check_vma=False)
```

time: 351 us -> 291 us (0.83)
  other arithmetic: 56.6 us -> 14.8 us
  waiting for transfers between devices: 139 us -> 107 us
  Pallas kernels: 69.6 us -> 96 us
  local copies, waits for them, and re-layouts: 32.5 us -> 21 us
  starting transfers between devices: 39.2 us -> 42.9 us
    ppermute x14 -> x16, waiting for transfers between devices: 72.1 us -> 43.7 us  [across(): return lax.ppermute(values, 'tensor', [(0, 1), (1, 0)])]
    pallas_call x9 -> x32, Pallas kernels: 69.6 us -> 96 us  [call(): pl.pallas_call(kernel, grid_spec=pltpu.PrefetchScalarGridSpec(num_scalar_...]
    convert_element_type x22 -> x5, other arithmetic: 17.3 us -> 1.93 us  [the longest x1 1.23 us: shards(): result = result.astype(BF16)]
    reduce_sum x8 -> x0, other arithmetic: 13.2 us -> none  [the longest x2 3.98 us: norm_rows(): return centred * lax.rsqrt(spread + 1e-05) * norm_gain + norm_offset]
    dynamic_slice x15 -> x1, local copies, waits for them, and re-layouts: 9.03 us -> 0.24 us  [slabs(): lax.dynamic_slice_in_dim(values, which * half, half, 1)]
    select_n x16 -> x1, other arithmetic: 8.02 us -> 1.01 us  [join(): jnp.where(which == 0, own, other)]
    concatenate x3 -> x1, other arithmetic: 6.49 us -> 0.02 us  [shards(): jnp.concatenate([one_sums[:2], two_sums[2:3], two_sums[:2], two_sums[3:4]])]
    ppermute x14 -> x16, starting transfers between devices: 13.4 us -> 18.7 us  [across(): return lax.ppermute(values, 'tensor', [(0, 1), (1, 0)])]
  transfers between devices with their start and end apart: 43 -> 45, of which waited for: 22 -> 23; matrix products, arithmetic and copies ran while one was open for 13% -> 10% of each run, Pallas kernels for 15% -> 25%
where the time goes in v2:
time: 291 us; the launch traced here: 290 us
  waiting for transfers between devices  107 us (37%)
  Pallas kernels  96 us (33%)
  starting transfers between devices  42.9 us (15%)
  local copies, waits for them, and re-layouts  21 us (7%)
  other arithmetic  14.8 us (5%)
  matrix products  6.4 us (2%)
    pallas_call x32, Pallas kernels, call(): pl.pallas_call(kernel, grid_spec=pltpu.PrefetchScalarGridSpec(num_scalar_...  96 us
    ppermute x29, waiting for transfers between devices, flip(): lax.ppermute(values, 'dp', [(d, d ^ bit) for d in range(lax.axis_size('dp...  62.8 us
    ppermute x16, waiting for transfers between devices, across(): return lax.ppermute(values, 'tensor', [(0, 1), (1, 0)])  43.7 us
    ppermute x29, starting transfers between devices, flip(): lax.ppermute(values, 'dp', [(d, d ^ bit) for d in range(lax.axis_size('dp...  24.2 us
    ppermute x16, starting transfers between devices, across(): return lax.ppermute(values, 'tensor', [(0, 1), (1, 0)])  18.7 us
    unnamed x159, local copies, waits for them, and re-layouts  12.5 us
    dot_general x4, matrix products, dot(): return lax.dot_general(left, right, dims, preferred_element_type=F32)  6.4 us
  transfers between devices with their start and end apart: 45, of which 23 were waited for; matrix products, arithmetic and copies ran while one was open for 10% of the time, Pallas kernels for 25%

profile of v2, /device:TPU:0, one launch (start us, length us, event | category | flops | bytes accessed | tf_op | source)
XLA Modules:
  0.0 290.0 jit_solution(15506356993527245260)
XLA Ops:
  6.0 3.0 %collective-permute-start = (bf16[512,768]{1,0:T(8,128)(2,1)}, bf16[512,768]{1,0:T(8,128)(2,1)}, u32[]{:S(2)}, u32[]{:S(2)}) collective-permute-start(bf16[512,768]{1,0:T(8,128)(2,1)} %shard_map.331.x_ref), channel_id=1, source_target_pairs={{0,1},{1,0},{2,3},{3,2},{4,5},{5,4},{6,7},{7,6},{8,9},{9,8},{10,11... | collective-permute-start | bytes 2359304 | tf_op jit(solution)/shard_map/ppermute | solution.py:62
  9.5 3.9 %fusion.17 = s32[384]{0:T(512)S(1)} fusion(s32[]{:T(128)} %bitcast.5, s32[]{:T(128)} %bitcast.6, s32[]{:T(128)} %bitcast.7, s32[]{:T(128)} %bitcast.8, s32[]{:T(128)} %bitcast.10, s32[]{:T(128)} %bitcast.9), kind=kLoop, calls=%fused_computation.53 | loop fusion | flops 8064 | bytes 1560 | tf_op jit(solution)/shard_map/gather | solution.py:852
  20.6 11.7 %collective-permute-done.1.reused_got_ref = bf16[512,192]{1,0:T(8,128)(2,1)S(1)} collective-permute-done((bf16[512,192]{1,0:T(8,128)(2,1)S(1)}, bf16[512,192]{1,0:T(8,128)(2,1)S(1)}, u32[]{:S(2)}, u32[]{:S(2)}) %collective-permute-start.1) | collective-permute-done | bytes 196640 | tf_op jit(solution)/shard_map/ppermute | solution.py:62
  34.3 4.7 %shard_map.332 = (bf16[1024,384]{1,0:T(8,128)(2,1)S(1)}, bf16[1024,384]{1,0:T(8,128)(2,1)S(1)}, bf16[1024,384]{1,0:T(8,128)(2,1)S(1)}) custom-call(s32[3]{0:T(128)S(1)} %pad_add_fusion.scalars, bf16[512,768]{1,0:T(8,128)(2,1)} %shard_map.331.x_ref, bf16[512,768]{1,0:T(8,128)(2,1)} %collective-permute-done.x_got_ref, ...), custom_call_target="tpu_custom_call" | custom-call | flops 69000003584 | bytes 216000000 | tf_op jit(solution)/shard_map/pallas_call | solution.py:32
  39.1 10.6 %shard_map.333 = (bf16[2,512,384]{2,1,0:T(8,128)(2,1)S(1)}, f32[3,2,1024]{2,1,0:T(2,128)S(1)}) custom-call(s32[3]{0:T(128)S(1)} %pad_add_fusion.scalars, bf16[1024,384]{1,0:T(8,128)(2,1)S(1)} %get-tuple-element.193.q_ref, bf16[1024,384]{1,0:T(8,128)(2,1)S(1)} %get-tuple-element.194.k_ref, bf16[1024,384]{1,0:T(8,128)(2,1)S(1)} %get-tuple-element.195.v_ref), custom_call_target="tpu_custom_call" | custom-call | flops 172499992576 | bytes 540000000 | tf_op jit(solution)/shard_map/pallas_call | solution.py:32
  54.1 8.3 %collective-permute-done.4.got_ref = bf16[512,384]{1,0:T(8,128)(2,1)S(1)} collective-permute-done((bf16[512,384]{1,0:T(8,128)(2,1)}, bf16[512,384]{1,0:T(8,128)(2,1)S(1)}, u32[]{:S(2)}, u32[]{:S(2)}) %collective-permute-start.4) | collective-permute-done | bytes 393248 | tf_op jit(solution)/shard_map/ppermute | solution.py:62
  63.5 2.9 shard_map.334
  68.5 9.4 %shard_map.335 = (f32[512,768]{1,0:T(8,128)S(1)}, f32[512,768]{1,0:T(8,128)S(1)}, bf16[512,1536]{1,0:T(8,128)(2,1)S(1)}, bf16[512,1536]{1,0:T(8,128)(2,1)S(1)}, f32[1,1536]{1,0:T(1,128)S(1)}) custom-call(s32[3]{0:T(128)S(1)} %pad_add_fusion.scalars, bf16[512,768]{1,0:T(8,128)(2,1)} %get-tuple-element.206.normed_ref.refs_4_, bf16[512,768]{1,0:T(8,128)(2,1)S(1)} %copy-done.10, ...), custom_call_target="tpu_custom_call" | custom-call | flops 172499992576 | bytes 540000000 | tf_op jit(solution)/shard_map/pallas_call | solution.py:32
  78.8 15.6 %collective-permute-done.6.normed_ref.refs_5_ = bf16[512,768]{1,0:T(8,128)(2,1)} collective-permute-done((bf16[512,768]{1,0:T(8,128)(2,1)}, bf16[512,768]{1,0:T(8,128)(2,1)}, u32[]{:S(2)}, u32[]{:S(2)}) %collective-permute-start.6) | collective-permute-done | bytes 786464 | tf_op jit(solution)/shard_map/ppermute | solution.py:62
  95.7 10.3 %shard_map.336 = (bf16[512,768]{1,0:T(8,128)(2,1)S(1)}, bf16[512,768]{1,0:T(8,128)(2,1)}, bf16[512,1536]{1,0:T(8,128)(2,1)S(1)}, bf16[512,1536]{1,0:T(8,128)(2,1)S(1)}, f32[1,1536]{1,0:T(1,128)S(1)}) custom-call(s32[3]{0:T(128)S(1)} %pad_add_fusion.scalars, bf16[512,768]{1,0:T(8,128)(2,1)} %collective-permute-done.6.normed_ref.refs_5_, ...), custom_call_target="tpu_custom_call" | custom-call | flops 172499992576 | bytes 540000000 | tf_op jit(solution)/shard_map/pallas_call | solution.py:32
  108.7 9.6 %shard_map.337 = (bf16[1,768,768]{2,1,0:T(8,128)(2,1)S(1)}, bf16[1,768,768]{2,1,0:T(8,128)(2,1)S(1)}, bf16[1,768,768]{2,1,0:T(8,128)(2,1)S(1)}, bf16[1,768,768]{2,1,0:T(8,128)(2,1)S(1)}) custom-call(s32[3]{0:T(128)S(1)} %pad_add_fusion.scalars, bf16[512,1536]{1,0:T(8,128)(2,1)S(1)} %get-tuple-element.214.refs_0_, ...), custom_call_target="tpu_custom_call" | custom-call | flops 172499992576 | bytes 540000000 | tf_op jit(solution)/shard_map/pallas_call | solution.py:32
  118.3 7.2 %collective-permute-done.8.back_got_ref = bf16[512,768]{1,0:T(8,128)(2,1)} collective-permute-done((bf16[512,768]{1,0:T(8,128)(2,1)}, bf16[512,768]{1,0:T(8,128)(2,1)}, u32[]{:S(2)}, u32[]{:S(2)}) %collective-permute-start.8) | collective-permute-done | bytes 786464 | tf_op jit(solution)/shard_map/ppermute | solution.py:62
  126.1 4.2 %shard_map.340 = (f32[512,768]{1,0:T(8,128)S(1)}, bf16[512,768]{1,0:T(8,128)(2,1)S(1)}, bf16[512,384]{1,0:T(8,128)(2,1)S(1)}, bf16[512,384]{1,0:T(8,128)(2,1)S(1)}, f32[8,768]{1,0:T(8,128)S(1)}) custom-call(s32[3]{0:T(128)S(1)} %pad_add_fusion.scalars, f32[512,768]{1,0:T(8,128)S(1)} %get-tuple-element.235.mid_ref, bf16[512,768]{1,0:T(8,128)(2,1)S(1)} %copy-done.2, ...), custom_call_target="tpu_custom_call" | custom-call | flops 69000003584 | bytes 216000000 | tf_op jit(solution)/shard_map/pallas_call | solution.py:32
  140.1 9.5 %collective-permute-done.11.refs_0_ = bf16[1,384,768]{2,1,0:T(8,128)(2,1)} collective-permute-done((bf16[1,384,768]{2,1,0:T(8,128)(2,1)}, bf16[1,384,768]{2,1,0:T(8,128)(2,1)}, u32[]{:S(2)}, u32[]{:S(2)}) %collective-permute-start.11) | collective-permute-done | bytes 589856 | tf_op jit(solution)/shard_map/ppermute | solution.py:66
  156.5 13.6 %shard_map.344 = (bf16[1024,384]{1,0:T(8,128)(2,1)S(1)}, bf16[1024,384]{1,0:T(8,128)(2,1)S(1)}, bf16[1024,384]{1,0:T(8,128)(2,1)S(1)}) custom-call(s32[3]{0:T(128)S(1)} %pad_add_fusion.scalars, bf16[1024,384]{1,0:T(8,128)(2,1)S(1)} %copy-done.51, bf16[1024,384]{1,0:T(8,128)(2,1)S(1)} %copy-done.53, bf16[1024,384]{1,0:T(8,128)(2,1)S(1)} %copy-done.55, ...), custom_call_target="tpu_custom_call" | custom-call | flops 241499996160 | bytes 756000000 | tf_op jit(solution)/shard_map/pallas_call | solution.py:32
  172.5 4.7 %shard_map.346 = (bf16[1,384,1408]{2,1,0:T(8,128)(2,1)S(1)}, bf16[1,384,1408]{2,1,0:T(8,128)(2,1)S(1)}, f32[1,384]{1,0:T(1,128)S(1)}, f32[1,192]{1,0:T(1,128)S(1)}) custom-call(s32[3]{0:T(128)S(1)} %pad_add_fusion.scalars, bf16[512,768]{1,0:T(8,128)(2,1)} %shard_map.331.x_ref, bf16[512,768]{1,0:T(8,128)(2,1)} %collective-permute-done.x_got_ref, ...), custom_call_target="tpu_custom_call" | custom-call | flops 69000003584 | bytes 216000000 | tf_op jit(solution)/shard_map/pallas_call | solution.py:32
  177.2 2.7 collective-permute-start.16
  180.9 3.0 %shard_map.348 = (f32[512,768]{1,0:T(8,128)S(1)}, bf16[512,768]{1,0:T(8,128)(2,1)S(1)}, bf16[512,192]{1,0:T(8,128)(2,1)S(1)}, bf16[512,192]{1,0:T(8,128)(2,1)S(1)}) custom-call(s32[3]{0:T(128)S(1)} %pad_add_fusion.scalars, bf16[1024,384]{1,0:T(8,128)(2,1)S(1)} %get-tuple-element.282.dq_ref.refs_0_.refs_3_, ...), custom_call_target="tpu_custom_call" | custom-call | flops 69000003584 | bytes 216000000 | tf_op jit(solution)/shard_map/pallas_call | solution.py:32
  185.4 4.5 %collective-permute-done.17.refs_0_ = bf16[1,192,768]{2,1,0:T(8,128)(2,1)S(1)} collective-permute-done((bf16[1,192,768]{2,1,0:T(8,128)(2,1)S(1)}, bf16[1,192,768]{2,1,0:T(8,128)(2,1)S(1)}, u32[]{:S(2)}, u32[]{:S(2)}) %collective-permute-start.17) | collective-permute-done | bytes 294944 | tf_op jit(solution)/shard_map/ppermute | solution.py:66
  194.4 2.9 %collective-permute-start.21 = (bf16[1,96,768]{2,1,0:T(8,128)(2,1)}, bf16[1,96,768]{2,1,0:T(8,128)(2,1)S(1)}, u32[]{:S(2)}, u32[]{:S(2)}) collective-permute-start(bf16[1,96,768]{2,1,0:T(8,128)(2,1)} %get-tuple-element.292), channel_id=1, source_target_pairs={{0,16},{2,18},{4,20},{6,22},{8,24},{10,26},{12,28},{14,30},{16,0},... | collective-permute-start | bytes 442376 | tf_op jit(solution)/shard_map/ppermute | solution.py:66
  198.5 5.8 %collective-permute-done.20.refs_1_ = bf16[1,96,768]{2,1,0:T(8,128)(2,1)S(1)} collective-permute-done((bf16[1,96,768]{2,1,0:T(8,128)(2,1)S(1)}, bf16[1,96,768]{2,1,0:T(8,128)(2,1)S(1)}, u32[]{:S(2)}, u32[]{:S(2)}) %collective-permute-start.20) | collective-permute-done | bytes 147488 | tf_op jit(solution)/shard_map/ppermute | solution.py:66
  204.3 3.0 %collective-permute-done.21 = bf16[1,96,768]{2,1,0:T(8,128)(2,1)S(1)} collective-permute-done((bf16[1,96,768]{2,1,0:T(8,128)(2,1)}, bf16[1,96,768]{2,1,0:T(8,128)(2,1)S(1)}, u32[]{:S(2)}, u32[]{:S(2)}) %collective-permute-start.21) | collective-permute-done | bytes 147488 | tf_op jit(solution)/shard_map/ppermute | solution.py:66
  207.3 3.1 %collective-permute-done.22.refs_0_ = bf16[1,192,1408]{2,1,0:T(8,128)(2,1)S(1)} collective-permute-done((bf16[1,192,1408]{2,1,0:T(8,128)(2,1)}, bf16[1,192,1408]{2,1,0:T(8,128)(2,1)S(1)}, u32[]{:S(2)}, u32[]{:S(2)}) %collective-permute-start.22) | collective-permute-done | bytes 540704 | tf_op jit(solution)/shard_map/ppermute | solution.py:66
  219.5 5.9 %collective-permute-done.26.refs_0_ = bf16[1,96,1408]{2,1,0:T(8,128)(2,1)S(1)} collective-permute-done((bf16[1,96,1408]{2,1,0:T(8,128)(2,1)}, bf16[1,96,1408]{2,1,0:T(8,128)(2,1)S(1)}, u32[]{:S(2)}, u32[]{:S(2)}) %collective-permute-start.26) | collective-permute-done | bytes 270368 | tf_op jit(solution)/shard_map/ppermute | solution.py:66
  225.5 3.7 %collective-permute-done.24.refs_1_ = bf16[1,192,768]{2,1,0:T(8,128)(2,1)S(1)} collective-permute-done((bf16[1,192,768]{2,1,0:T(8,128)(2,1)S(1)}, bf16[1,192,768]{2,1,0:T(8,128)(2,1)S(1)}, u32[]{:S(2)}, u32[]{:S(2)}) %collective-permute-start.24) | collective-permute-done | bytes 294944 | tf_op jit(solution)/shard_map/ppermute | solution.py:66
  233.8 2.9 shard_map.356
  240.3 4.9 %collective-permute-done.29.refs_1_ = bf16[1,384,768]{2,1,0:T(8,128)(2,1)S(1)} collective-permute-done((bf16[1,384,768]{2,1,0:T(8,128)(2,1)S(1)}, bf16[1,384,768]{2,1,0:T(8,128)(2,1)S(1)}, u32[]{:S(2)}, u32[]{:S(2)}) %collective-permute-start.29) | collective-permute-done | bytes 589856 | tf_op jit(solution)/shard_map/ppermute | solution.py:66
  251.3 3.0 %fusion = f32[512,768]{1,0:T(8,128)} fusion(bf16[768,384]{1,0:T(8,128)(2,1)} %copy-done.58, bf16[512,192]{1,0:T(8,128)(2,1)} %get-tuple-element.365, bf16[512,192]{1,0:T(8,128)(2,1)} %get-tuple-element.364), kind=kOutput, calls=%fused_computation.8 | convolution fusion | flops 302776320 | bytes 2555904 | tf_op jit(solution)/shard_map/dot_general | solution.py:54
  254.4 4.9 %collective-permute-done.34.refs_1_ = bf16[1,384,768]{2,1,0:T(8,128)(2,1)} collective-permute-done((bf16[1,384,768]{2,1,0:T(8,128)(2,1)}, bf16[1,384,768]{2,1,0:T(8,128)(2,1)}, u32[]{:S(2)}, u32[]{:S(2)}) %collective-permute-start.34) | collective-permute-done | bytes 589856 | tf_op jit(solution)/shard_map/ppermute | solution.py:66
  270.9 6.1 %shard_map.361 = (f32[1536,768]{1,0:T(8,128)}, f32[768,1536]{1,0:T(8,128)}) custom-call(s32[3]{0:T(128)S(1)} %pad_add_fusion.scalars, bf16[1,768,768]{2,1,0:T(8,128)(2,1)S(1)} %shard_map.354.refs_0_, bf16[1,768,768]{2,1,0:T(8,128)(2,1)} %collective-permute-done.33.refs_1_, bf16[1,768,768]{2,1,0:T(8,128)(2,1)S(1)} %shard_map.357.refs_2_, ...), custom_call_target="tpu_custom_call" | custom-call | flops 86249996288 | bytes 270000000 | tf_op jit(solution)/shard_map/pallas_call | solution.py:32
  277.0 7.4 %collective-permute-done.42.refs_1_ = bf16[1,192,1408]{2,1,0:T(8,128)(2,1)S(1)} collective-permute-done((bf16[1,192,1408]{2,1,0:T(8,128)(2,1)S(1)}, bf16[1,192,1408]{2,1,0:T(8,128)(2,1)S(1)}, u32[]{:S(2)}, u32[]{:S(2)}) %collective-permute-start.42) | collective-permute-done | bytes 540704 | tf_op jit(solution)/shard_map/ppermute | solution.py:66
  287.2 2.7 shard_map.362
  (303 shorter events, 91.9 us)
Async XLA Ops:
  6.0 26.3 %collective-permute-start = (bf16[512,768]{1,0:T(8,128)(2,1)}, bf16[512,768]{1,0:T(8,128)(2,1)}, u32[]{:S(2)}, u32[]{:S(2)}) collective-permute-start(bf16[512,768]{1,0:T(8,128)(2,1)} %shard_map.331.x_ref), channel_id=1, source_target_pairs={{0,1},{1,0},{2,3},{3,2},{4,5},{5,4},{6,7},{7,6},{8,9},{9,8},{10,11... | collective-permute-start | bytes 2359304 | tf_op jit(solution)/shard_map/ppermute | solution.py:62
  14.6 17.7 %collective-permute-start.1 = (bf16[512,192]{1,0:T(8,128)(2,1)S(1)}, bf16[512,192]{1,0:T(8,128)(2,1)S(1)}, u32[]{:S(2)}, u32[]{:S(2)}) collective-permute-start(bf16[512,192]{1,0:T(8,128)(2,1)S(1)} %get-tuple-element.367), channel_id=1, source_target_pairs={{0,1},{1,0},{2,3},{3,2},{4,5},{5,4},{6,7},{7,6},{8,9},{9,8},{10,11... | collective-permute-start | bytes 589832 | tf_op jit(solution)/shard_map/ppermute | solution.py:62
  32.3 17.4 %collective-permute-start.2 = (bf16[192,768]{1,0:T(8,128)(2,1)}, bf16[192,768]{1,0:T(8,128)(2,1)}, u32[]{:S(2)}, u32[]{:S(2)}) collective-permute-start(bf16[192,768]{1,0:T(8,128)(2,1)} %constant_dynamic-slice_fusion.1), channel_id=1, source_target_pairs={{0,1},{1,0},{2,3},{3,2},{4,5},{5,4},{6,7},{7,6},{8,9},{9,8},{10,11... | collective-permute-start | bytes 884744 | tf_op jit(solution)/shard_map/ppermute | solution.py:62
  34.0 15.7 %collective-permute-start.3 = (bf16[256,768]{1,0:T(8,128)(2,1)}, bf16[256,768]{1,0:T(8,128)(2,1)}, u32[]{:S(2)}, u32[]{:S(2)}) collective-permute-start(bf16[256,768]{1,0:T(8,128)(2,1)} %get-tuple-element.198), channel_id=1, source_target_pairs={{0,1},{1,0},{2,3},{3,2},{4,5},{5,4},{6,7},{7,6},{8,9},{9,8},{10,11... | collective-permute-start | bytes 1179656 | tf_op jit(solution)/shard_map/ppermute | solution.py:62
  50.6 11.7 %collective-permute-start.4 = (bf16[512,384]{1,0:T(8,128)(2,1)}, bf16[512,384]{1,0:T(8,128)(2,1)S(1)}, u32[]{:S(2)}, u32[]{:S(2)}) collective-permute-start(bf16[512,384]{1,0:T(8,128)(2,1)} %slice_bitcast_fusion), channel_id=1, source_target_pairs={{0,1},{1,0},{2,3},{3,2},{4,5},{5,4},{6,7},{7,6},{8,9},{9,8},{10,11... | collective-permute-start | bytes 1179656 | tf_op jit(solution)/shard_map/ppermute | solution.py:62
  66.4 12.4 %collective-permute-start.7 = (bf16[256,768]{1,0:T(8,128)(2,1)}, bf16[256,768]{1,0:T(8,128)(2,1)}, u32[]{:S(2)}, u32[]{:S(2)}) collective-permute-start(bf16[256,768]{1,0:T(8,128)(2,1)} %get-tuple-element.207), channel_id=1, source_target_pairs={{0,1},{1,0},{2,3},{3,2},{4,5},{5,4},{6,7},{7,6},{8,9},{9,8},{10,11... | collective-permute-start | bytes 1179656 | tf_op jit(solution)/shard_map/ppermute | solution.py:62
  68.2 26.2 %collective-permute-start.6 = (bf16[512,768]{1,0:T(8,128)(2,1)}, bf16[512,768]{1,0:T(8,128)(2,1)}, u32[]{:S(2)}, u32[]{:S(2)}) collective-permute-start(bf16[512,768]{1,0:T(8,128)(2,1)} %get-tuple-element.206.normed_ref.refs_4_), channel_id=1, source_target_pairs={{0,1},{1,0},{2,3},{3,2},{4,5},{5,4},{6,7},{7,6},{8,9},{9,8},{10,11... | collective-permute-start | bytes 2359304 | tf_op jit(solution)/shard_map/ppermute | solution.py:62
  106.9 18.6 %collective-permute-start.8 = (bf16[512,768]{1,0:T(8,128)(2,1)}, bf16[512,768]{1,0:T(8,128)(2,1)}, u32[]{:S(2)}, u32[]{:S(2)}) collective-permute-start(bf16[512,768]{1,0:T(8,128)(2,1)} %get-tuple-element.225), channel_id=1, source_target_pairs={{0,1},{1,0},{2,3},{3,2},{4,5},{5,4},{6,7},{7,6},{8,9},{9,8},{10,11... | collective-permute-start | bytes 2359304 | tf_op jit(solution)/shard_map/ppermute | solution.py:62
  134.1 15.6 %collective-permute-start.11 = (bf16[1,384,768]{2,1,0:T(8,128)(2,1)}, bf16[1,384,768]{2,1,0:T(8,128)(2,1)}, u32[]{:S(2)}, u32[]{:S(2)}) collective-permute-start(bf16[1,384,768]{2,1,0:T(8,128)(2,1)} %get-tuple-element.244), channel_id=1, source_target_pairs={{0,4},{2,6},{4,0},{6,2},{8,12},{10,14},{12,8},{14,10},{16,20},{18,... | collective-permute-start | bytes 1769480 | tf_op jit(solution)/shard_map/ppermute | solution.py:66
  135.8 15.9 %collective-permute-start.12 = (bf16[512,384]{1,0:T(8,128)(2,1)}, bf16[512,384]{1,0:T(8,128)(2,1)S(1)}, u32[]{:S(2)}, u32[]{:S(2)}) collective-permute-start(bf16[512,384]{1,0:T(8,128)(2,1)} %copy-done.32), channel_id=1, source_target_pairs={{0,1},{1,0},{2,3},{3,2},{4,5},{5,4},{6,7},{7,6},{8,9},{9,8},{10,11... | collective-permute-start | bytes 1179656 | tf_op jit(solution)/shard_map/ppermute | solution.py:62
  151.7 18.4 %collective-permute-start.13 = (bf16[1,192,768]{2,1,0:T(8,128)(2,1)}, bf16[1,192,768]{2,1,0:T(8,128)(2,1)}, u32[]{:S(2)}, u32[]{:S(2)}) collective-permute-start(bf16[1,192,768]{2,1,0:T(8,128)(2,1)} %get-tuple-element.252), channel_id=1, source_target_pairs={{0,8},{2,10},{4,12},{6,14},{8,0},{10,2},{12,4},{14,6},{16,24},{18,... | collective-permute-start | bytes 884744 | tf_op jit(solution)/shard_map/ppermute | solution.py:66
  153.5 17.8 %collective-permute-start.14 = (bf16[1,384,768]{2,1,0:T(8,128)(2,1)}, bf16[1,384,768]{2,1,0:T(8,128)(2,1)}, u32[]{:S(2)}, u32[]{:S(2)}) collective-permute-start(bf16[1,384,768]{2,1,0:T(8,128)(2,1)} %get-tuple-element.256), channel_id=1, source_target_pairs={{0,4},{2,6},{4,0},{6,2},{8,12},{10,14},{12,8},{14,10},{16,20},{18,... | collective-permute-start | bytes 1769480 | tf_op jit(solution)/shard_map/ppermute | solution.py:66
  154.9 17.5 %collective-permute-start.15 = (bf16[384,768]{1,0:T(8,128)(2,1)}, bf16[384,768]{1,0:T(8,128)(2,1)}, u32[]{:S(2)}, u32[]{:S(2)}) collective-permute-start(bf16[384,768]{1,0:T(8,128)(2,1)} %convolution_convert_fusion), channel_id=1, source_target_pairs={{0,1},{1,0},{2,3},{3,2},{4,5},{5,4},{6,7},{7,6},{8,9},{9,8},{10,11... | collective-permute-start | bytes 1769480 | tf_op jit(solution)/shard_map/ppermute | solution.py:62
  177.2 8.2 %collective-permute-start.16 = (bf16[1,96,768]{2,1,0:T(8,128)(2,1)S(1)}, bf16[1,96,768]{2,1,0:T(8,128)(2,1)S(1)}, u32[]{:S(2)}, u32[]{:S(2)}) collective-permute-start(bf16[1,96,768]{2,1,0:T(8,128)(2,1)S(1)} %get-tuple-element.268), channel_id=1, source_target_pairs={{0,16},{2,18},{4,20},{6,22},{8,24},{10,26},{12,28},{14,30},{16,0},... | collective-permute-start | bytes 442376 | tf_op jit(solution)/shard_map/ppermute | solution.py:66
  179.8 10.0 %collective-permute-start.17 = (bf16[1,192,768]{2,1,0:T(8,128)(2,1)S(1)}, bf16[1,192,768]{2,1,0:T(8,128)(2,1)S(1)}, u32[]{:S(2)}, u32[]{:S(2)}) collective-permute-start(bf16[1,192,768]{2,1,0:T(8,128)(2,1)S(1)} %get-tuple-element.270), channel_id=1, source_target_pairs={{0,8},{2,10},{4,12},{6,14},{8,0},{10,2},{12,4},{14,6},{16,24},{18,... | collective-permute-start | bytes 884744 | tf_op jit(solution)/shard_map/ppermute | solution.py:66
  180.3 12.1 %collective-permute-start.19 = (bf16[256,768]{1,0:T(8,128)(2,1)S(1)}, bf16[256,768]{1,0:T(8,128)(2,1)S(1)}, u32[]{:S(2)}, u32[]{:S(2)}) collective-permute-start(bf16[256,768]{1,0:T(8,128)(2,1)S(1)} %slice.67), channel_id=1, source_target_pairs={{0,1},{1,0},{2,3},{3,2},{4,5},{5,4},{6,7},{7,6},{8,9},{9,8},{10,11... | collective-permute-start | bytes 1179656 | tf_op jit(solution)/shard_map/ppermute | solution.py:62
  180.9 9.7 %collective-permute-start.18 = (bf16[1,384,1408]{2,1,0:T(8,128)(2,1)S(1)}, bf16[1,384,1408]{2,1,0:T(8,128)(2,1)S(1)}, u32[]{:S(2)}, u32[]{:S(2)}) collective-permute-start(bf16[1,384,1408]{2,1,0:T(8,128)(2,1)S(1)} %get-tuple-element.279), channel_id=1, source_target_pairs={{0,2},{2,0},{4,6},{6,4},{8,10},{10,8},{12,14},{14,12},{16,18},{18,... | collective-permute-start | bytes 3244040 | tf_op jit(solution)/shard_map/ppermute | solution.py:66
  193.2 11.1 %collective-permute-start.20 = (bf16[1,96,768]{2,1,0:T(8,128)(2,1)S(1)}, bf16[1,96,768]{2,1,0:T(8,128)(2,1)S(1)}, u32[]{:S(2)}, u32[]{:S(2)}) collective-permute-start(bf16[1,96,768]{2,1,0:T(8,128)(2,1)S(1)} %add_convert_fusion.1.refs_0_), channel_id=1, source_target_pairs={{0,16},{2,18},{4,20},{6,22},{8,24},{10,26},{12,28},{14,30},{16,0},... | collective-permute-start | bytes 442376 | tf_op jit(solution)/shard_map/ppermute | solution.py:66
  194.4 12.9 %collective-permute-start.21 = (bf16[1,96,768]{2,1,0:T(8,128)(2,1)}, bf16[1,96,768]{2,1,0:T(8,128)(2,1)S(1)}, u32[]{:S(2)}, u32[]{:S(2)}) collective-permute-start(bf16[1,96,768]{2,1,0:T(8,128)(2,1)} %get-tuple-element.292), channel_id=1, source_target_pairs={{0,16},{2,18},{4,20},{6,22},{8,24},{10,26},{12,28},{14,30},{16,0},... | collective-permute-start | bytes 442376 | tf_op jit(solution)/shard_map/ppermute | solution.py:66
  197.4 14.6 %collective-permute-start.23 = (bf16[256,768]{1,0:T(8,128)(2,1)S(1)}, bf16[256,768]{1,0:T(8,128)(2,1)S(1)}, u32[]{:S(2)}, u32[]{:S(2)}) collective-permute-start(bf16[256,768]{1,0:T(8,128)(2,1)S(1)} %slice.68), channel_id=1, source_target_pairs={{0,1},{1,0},{2,3},{3,2},{4,5},{5,4},{6,7},{7,6},{8,9},{9,8},{10,11... | collective-permute-start | bytes 1179656 | tf_op jit(solution)/shard_map/ppermute | solution.py:62
  197.9 12.5 %collective-permute-start.22 = (bf16[1,192,1408]{2,1,0:T(8,128)(2,1)}, bf16[1,192,1408]{2,1,0:T(8,128)(2,1)S(1)}, u32[]{:S(2)}, u32[]{:S(2)}) collective-permute-start(bf16[1,192,1408]{2,1,0:T(8,128)(2,1)} %copy-done.30), channel_id=1, source_target_pairs={{0,4},{2,6},{4,0},{6,2},{8,12},{10,14},{12,8},{14,10},{16,20},{18,... | collective-permute-start | bytes 1622024 | tf_op jit(solution)/shard_map/ppermute | solution.py:66
  214.2 15.0 %collective-permute-start.28 = (bf16[512,192]{1,0:T(8,128)(2,1)}, bf16[512,192]{1,0:T(8,128)(2,1)S(1)}, u32[]{:S(2)}, u32[]{:S(2)}) collective-permute-start(bf16[512,192]{1,0:T(8,128)(2,1)} %copy-done.36), channel_id=1, source_target_pairs={{0,1},{1,0},{2,3},{3,2},{4,5},{5,4},{6,7},{7,6},{8,9},{9,8},{10,11... | collective-permute-start | bytes 589832 | tf_op jit(solution)/shard_map/ppermute | solution.py:62
  215.8 9.6 %collective-permute-start.26 = (bf16[1,96,1408]{2,1,0:T(8,128)(2,1)}, bf16[1,96,1408]{2,1,0:T(8,128)(2,1)S(1)}, u32[]{:S(2)}, u32[]{:S(2)}) collective-permute-start(bf16[1,96,1408]{2,1,0:T(8,128)(2,1)} %copy-done.35), channel_id=1, source_target_pairs={{0,8},{2,10},{4,12},{6,14},{8,0},{10,2},{12,4},{14,6},{16,24},{18,... | collective-permute-start | bytes 811016 | tf_op jit(solution)/shard_map/ppermute | solution.py:66
  215.8 13.4 %collective-permute-start.24 = (bf16[1,192,768]{2,1,0:T(8,128)(2,1)S(1)}, bf16[1,192,768]{2,1,0:T(8,128)(2,1)S(1)}, u32[]{:S(2)}, u32[]{:S(2)}) collective-permute-start(bf16[1,192,768]{2,1,0:T(8,128)(2,1)S(1)} %shard_map.349.refs_0_), channel_id=1, source_target_pairs={{0,8},{2,10},{4,12},{6,14},{8,0},{10,2},{12,4},{14,6},{16,24},{18,... | collective-permute-start | bytes 884744 | tf_op jit(solution)/shard_map/ppermute | solution.py:66
  217.8 11.4 %collective-permute-start.27 = (bf16[256,768]{1,0:T(8,128)(2,1)S(1)}, bf16[256,768]{1,0:T(8,128)(2,1)S(1)}, u32[]{:S(2)}, u32[]{:S(2)}) collective-permute-start(bf16[256,768]{1,0:T(8,128)(2,1)S(1)} %slice.69), channel_id=1, source_target_pairs={{0,1},{1,0},{2,3},{3,2},{4,5},{5,4},{6,7},{7,6},{8,9},{9,8},{10,11... | collective-permute-start | bytes 1179656 | tf_op jit(solution)/shard_map/ppermute | solution.py:62
  231.2 8.2 %collective-permute-start.30 = (bf16[1,192,768]{2,1,0:T(8,128)(2,1)S(1)}, bf16[1,192,768]{2,1,0:T(8,128)(2,1)S(1)}, u32[]{:S(2)}, u32[]{:S(2)}) collective-permute-start(bf16[1,192,768]{2,1,0:T(8,128)(2,1)S(1)} %shard_map.352.refs_0_), channel_id=1, source_target_pairs={{0,8},{2,10},{4,12},{6,14},{8,0},{10,2},{12,4},{14,6},{16,24},{18,... | collective-permute-start | bytes 884744 | tf_op jit(solution)/shard_map/ppermute | solution.py:66
  231.9 13.4 %collective-permute-start.32 = (bf16[256,768]{1,0:T(8,128)(2,1)S(1)}, bf16[256,768]{1,0:T(8,128)(2,1)S(1)}, u32[]{:S(2)}, u32[]{:S(2)}) collective-permute-start(bf16[256,768]{1,0:T(8,128)(2,1)S(1)} %slice.70), channel_id=1, source_target_pairs={{0,1},{1,0},{2,3},{3,2},{4,5},{5,4},{6,7},{7,6},{8,9},{9,8},{10,11... | collective-permute-start | bytes 1179656 | tf_op jit(solution)/shard_map/ppermute | solution.py:62
  233.3 11.9 %collective-permute-start.29 = (bf16[1,384,768]{2,1,0:T(8,128)(2,1)S(1)}, bf16[1,384,768]{2,1,0:T(8,128)(2,1)S(1)}, u32[]{:S(2)}, u32[]{:S(2)}) collective-permute-start(bf16[1,384,768]{2,1,0:T(8,128)(2,1)S(1)} %shard_map.351.refs_0_), channel_id=1, source_target_pairs={{0,4},{2,6},{4,0},{6,2},{8,12},{10,14},{12,8},{14,10},{16,20},{18,... | collective-permute-start | bytes 1769480 | tf_op jit(solution)/shard_map/ppermute | solution.py:66
  246.5 7.8 %collective-permute-start.35 = (bf16[1,48,1408]{2,1,0:T(8,128)(2,1)S(1)}, bf16[1,48,1408]{2,1,0:T(8,128)(2,1)S(1)}, u32[]{:S(2)}, u32[]{:S(2)}) collective-permute-start(bf16[1,48,1408]{2,1,0:T(8,128)(2,1)S(1)} %add_convert_fusion.2.refs_0_), channel_id=1, source_target_pairs={{0,16},{2,18},{4,20},{6,22},{8,24},{10,26},{12,28},{14,30},{16,0},... | collective-permute-start | bytes 405512 | tf_op jit(solution)/shard_map/ppermute | solution.py:66
  248.4 11.0 %collective-permute-start.34 = (bf16[1,384,768]{2,1,0:T(8,128)(2,1)}, bf16[1,384,768]{2,1,0:T(8,128)(2,1)}, u32[]{:S(2)}, u32[]{:S(2)}) collective-permute-start(bf16[1,384,768]{2,1,0:T(8,128)(2,1)} %copy-done.28), channel_id=1, source_target_pairs={{0,4},{2,6},{4,0},{6,2},{8,12},{10,14},{12,8},{14,10},{16,20},{18,... | collective-permute-start | bytes 1769480 | tf_op jit(solution)/shard_map/ppermute | solution.py:66
  248.9 11.6 %collective-permute-start.33 = (bf16[1,768,768]{2,1,0:T(8,128)(2,1)S(1)}, bf16[1,768,768]{2,1,0:T(8,128)(2,1)}, u32[]{:S(2)}, u32[]{:S(2)}) collective-permute-start(bf16[1,768,768]{2,1,0:T(8,128)(2,1)S(1)} %shard_map.354.refs_0_), channel_id=1, source_target_pairs={{0,2},{2,0},{4,6},{6,4},{8,10},{10,8},{12,14},{14,12},{16,18},{18,... | collective-permute-start | bytes 3538952 | tf_op jit(solution)/shard_map/ppermute | solution.py:66
  270.3 14.0 %collective-permute-start.42 = (bf16[1,192,1408]{2,1,0:T(8,128)(2,1)S(1)}, bf16[1,192,1408]{2,1,0:T(8,128)(2,1)S(1)}, u32[]{:S(2)}, u32[]{:S(2)}) collective-permute-start(bf16[1,192,1408]{2,1,0:T(8,128)(2,1)S(1)} %shard_map.359.refs_0_), channel_id=1, source_target_pairs={{0,4},{2,6},{4,0},{6,2},{8,12},{10,14},{12,8},{14,10},{16,20},{18,... | collective-permute-start | bytes 1622024 | tf_op jit(solution)/shard_map/ppermute | solution.py:66
  (92 other events, 716.2 us)
